TPU v7x, 256 devices: a whole 4x4x8 slice. The times are simulated.
256 devices in a mesh: row: 16 (over y, x), col: 16 (over z, core).
Axes of the slice: x: 4, y: 4, z: 8, core: 2. Of those that a mesh axis runs over, the one named last changes fastest.
Arguments:
- tokens: bfloat16 [512, 8192], P('col', 'row'), may hold values from -6 to 6
- gate_quant: bfloat16 [8192, 26624], P('row', 'col'), may hold values from -120 to 120, as said below
- gate_scale: float32 [64, 208], P('row', 'col'), as said below
- up_quant: bfloat16 [8192, 26624], P('row', 'col'), may hold values from -120 to 120, as said below
- up_scale: float32 [64, 208], P('row', 'col'), as said below
- down_quant: bfloat16 [26624, 8192], P('col', 'row'), may hold values from -120 to 120, as said below
- down_scale: float32 [208, 64], P('col', 'row'), as said below
- out_grad: bfloat16 [512, 8192], P('col', 'row'), may hold values from -6 to 6
Outputs:
- output: bfloat16 [512, 8192], P('col', 'row')
- input_grad: bfloat16 [512, 8192], P('col', 'row')
- gate_grad: bfloat16 [8192, 26624], P('row', 'col')
- up_grad: bfloat16 [8192, 26624], P('row', 'col')
- down_grad: bfloat16 [26624, 8192], P('col', 'row')
Inputs may be any that keep to these rules, and one draw needn't show every extreme that they name: `gate_quant`: every entry is a sign times a mantissa of 8 to 15 eighths times a power of two from 4 to 64. `up_quant`: every entry is a sign times a mantissa of 8 to 15 eighths times a power of two from 4 to 64. `down_quant`: every entry is a sign times a mantissa of 8 to 15 eighths times a power of two from 4 to 64. `gate_scale`: every entry is a positive power of two. `up_scale`: every entry is a positive power of two. `down_scale`: every entry is a positive power of two.
All inputs are finite; a program needn't handle non-finite values.
Results may differ from a plain program's by a relative error of at most 0.005.
Values may be sent and summed in bfloat16 or wider, within the bound.
No kernel may reach another device: no remote copies, remote signals or barrier semaphores. Data moves between devices by JAX's collectives and lax.ppermute only.
A program may use at most 128 MiB of HBM per device.

v0:
```python
import jax
import jax.numpy as jnp
from jax import lax
from jax.sharding import PartitionSpec as P


def dequantize(quantized, scales):
    block_rows, block_columns = scales.shape
    height, width = quantized.shape
    blocks = quantized.astype(jnp.float32).reshape(
        block_rows, height // block_rows, block_columns, width // block_columns
    )
    return (blocks * scales[:, None, :, None]).reshape(height, width).astype(jnp.bfloat16)


def matmul(left, right):
    return jnp.dot(left, right, preferred_element_type=jnp.float32)


def inner_first(left, right):
    return lax.dot_general(
        left, right, (((0,), (0,)), ((), ())), preferred_element_type=jnp.float32
    )


def inner_last(left, right):
    return lax.dot_general(
        left, right, (((1,), (1,)), ((), ())), preferred_element_type=jnp.float32
    )


def local(tokens, gate_quant, gate_scale, up_quant, up_scale, down_quant, down_scale, out_grad):
    w_gate = dequantize(gate_quant, gate_scale)
    w_up = dequantize(up_quant, up_scale)
    w_down = dequantize(down_quant, down_scale)
    panel = lax.all_gather(tokens, "col", axis=0, tiled=True)
    width = w_gate.shape[1]
    summed = lax.psum_scatter(
        jnp.concatenate([matmul(panel, w_gate), matmul(panel, w_up)], axis=1),
        "row",
        scatter_dimension=0,
        tiled=True,
    )
    gate = summed[:, :width]
    up = summed[:, width:]
    sigmoid_gate = jax.nn.sigmoid(gate)
    activated = gate * sigmoid_gate
    hidden_part = (activated * up).astype(jnp.bfloat16)
    hidden = lax.all_gather(hidden_part, "row", axis=0, tiled=True)
    output = lax.psum_scatter(
        matmul(hidden, w_down), "col", scatter_dimension=0, tiled=True
    ).astype(jnp.bfloat16)
    grad_panel = lax.all_gather(out_grad, "col", axis=0, tiled=True)
    down_grad = inner_first(hidden, grad_panel).astype(jnp.bfloat16)
    hidden_grad = lax.psum_scatter(
        inner_last(grad_panel, w_down), "row", scatter_dimension=0, tiled=True
    )
    pre_gate = (hidden_grad * up * sigmoid_gate * (1.0 + gate * (1.0 - sigmoid_gate))).astype(
        jnp.bfloat16
    )
    pre_up = (hidden_grad * activated).astype(jnp.bfloat16)
    pre_gate, pre_up = (
        lax.all_gather(pre_gate, "row", axis=0, tiled=True),
        lax.all_gather(pre_up, "row", axis=0, tiled=True),
    )
    piece = lax.all_gather(tokens, "col", axis=0, tiled=True)
    gate_piece = pre_gate
    up_piece = pre_up
    gate_total = inner_first(piece, gate_piece)
    up_total = inner_first(piece, up_piece)
    gate_grad = gate_total.astype(jnp.bfloat16)
    up_grad = up_total.astype(jnp.bfloat16)
    gate_piece = pre_gate
    up_piece = pre_up
    input_grad = lax.psum_scatter(
        inner_last(gate_piece, w_gate) + inner_last(up_piece, w_up),
        "col",
        scatter_dimension=0,
        tiled=True,
    ).astype(jnp.bfloat16)
    return (output, input_grad, gate_grad, up_grad, down_grad)


def solution(mesh):
    placed = (
        P("col", "row"),
        P("row", "col"),
        P("row", "col"),
        P("row", "col"),
        P("row", "col"),
        P("col", "row"),
        P("col", "row"),
        P("col", "row"),
    )
    return jax.shard_map(
        local,
        mesh=mesh,
        in_specs=placed,
        out_specs=(
            P("col", "row"),
            P("col", "row"),
            P("row", "col"),
            P("row", "col"),
            P("col", "row"),
        ),
        check_vma=False,
    )
```

profile of v0, /device:TPU:1, one launch (start us, length us, event | category | flops | bytes accessed | tf_op | source)
XLA Modules:
  0.0 487.3 jit_solution(8767121019165621667)
XLA Ops:
  7.2 0.0 reduce-scatter.15.cloned.1.call-start
  7.2 0.8 copy.39
  8.0 23.0 %all_gather.18 = bf16[512,512]{1,0:T(8,128)(2,1)S(1)} all-gather(bf16[32,512]{1,0:T(8,128)(2,1)} %param.15), channel_id=1, replica_groups=mesh['row'=16,'col'=16] {'col'}, dimensions={0}, use_global_device_ids=true | all-gather | bytes 557056 | tf_op jit(solution)/shard_map/all_gather | solution.py:53
  31.0 0.5 mul.62
  31.5 0.3 copy-done.7
  31.7 0.9 copy-done.4
  32.6 2.8 convolution_bitcast_fusion
  35.4 4.8 copy.46
  40.3 0.0 reduce-scatter.13.cloned.1.call-start
  40.3 0.6 copy-done.12
  40.9 0.1 copy.36
  41.0 3.6 copy.35
  44.7 0.1 copy.34
  44.8 3.6 copy.33
  48.4 15.9 %all_gather.16 = bf16[512,512]{1,0:T(8,128)(2,1)S(1)} all-gather(bf16[32,512]{1,0:T(8,128)(2,1)S(1)} %copy-done.11), channel_id=1, replica_groups=mesh['row'=16,'col'=16] {'col'}, dimensions={0}, use_global_device_ids=true | all-gather | bytes 557056 | tf_op jit(solution)/shard_map/all_gather | solution.py:36
  64.3 0.5 mul.57
  64.8 1.6 copy-done.2
  66.4 1.1 convolution_bitcast_fusion.1
  67.5 0.5 mul.54
  68.0 1.7 copy-done.1
  69.7 1.1 convolution_bitcast_fusion.2
  70.8 3.7 pad_maximum_fusion
  74.5 7.7 %copy.44 = f32[512,3328]{1,0:T(8,128)} copy(f32[512,3328]{0,1:T(8,128)} %pad_maximum_fusion) | data formatting | bytes 13631488
  82.2 0.0 all-gather.6.cloned.1.call-start
  82.3 35.3 %reduce-scatter.15.cloned.1.call-done = f32[32,1664]{1,0:T(8,128)} async-done(((f32[512,1664]{1,0:T(8,128)}), f32[32,1664]{1,0:T(8,128)}) %reduce-scatter.15.cloned.1.call-update) | async-done | bytes 213008 | tf_op jit(solution)/shard_map/reduce_scatter | solution.py:55
  117.6 91.0 %reduce-scatter.13.cloned.1.call-done = f32[32,3328]{1,0:T(8,128)} async-done(((f32[512,3328]{1,0:T(8,128)}), f32[32,3328]{1,0:T(8,128)}) %reduce-scatter.13.cloned.1.call-update) | async-done | bytes 426000 | tf_op jit(solution)/shard_map/reduce_scatter | solution.py:38
  208.6 2.0 multiply_convert_fusion
  210.6 0.0 all-gather.8.cloned.1.call-start
  210.6 0.5 all-gather.8.cloned.1.call-update
  211.2 0.0 all-gather.4.cloned.1.call-start
  211.2 0.5 all-gather.4.cloned.1.call-update
  211.8 0.0 reduce-scatter.11.cloned.1.call-start
  211.8 48.8 %all-gather.6.cloned.1.call-done = bf16[512,1664]{1,0:T(8,128)(2,1)} async-done(((bf16[32,1664]{1,0:T(8,128)(2,1)}), bf16[512,1664]{1,0:T(8,128)(2,1)}) %all-gather.6.cloned.1.call-update) | async-done | bytes 1703952 | tf_op jit(solution)/shard_map/all_gather | solution.py:63
  260.6 5.1 %fusion.6 = f32[512,512]{1,0:T(8,128)} fusion(bf16[512,1664]{1,0:T(8,128)(2,1)} %all-gather.6.cloned.1.call-done, f32[208,8,4,128]{3,2,1,0:T(4,128)} %bitcast.57, bf16[512,1664]{0,1:T(8,128)(2,1)} %copy.33), kind=kOutput, calls=%fused_computation.21 | convolution fusion | flops 874971136 | bytes 7864320 | tf_op jit(solution)/shard_map/dot_general | solution.py:27
  265.7 46.2 %all-gather.8.cloned.1.call-done = bf16[512,1664]{1,0:T(8,128)(2,1)} async-done(((bf16[32,1664]{1,0:T(8,128)(2,1)}), bf16[512,1664]{1,0:T(8,128)(2,1)}) %all-gather.8.cloned.1.call-update) | async-done | bytes 1703952 | tf_op jit(solution)/shard_map/all_gather | solution.py:64
  311.9 5.4 %convolution_add_fusion = f32[512,512]{1,0:T(8,128)} fusion(f32[512,512]{1,0:T(8,128)} %fusion.6, bf16[512,1664]{1,0:T(8,128)(2,1)} %all-gather.8.cloned.1.call-done, f32[208,8,4,128]{3,2,1,0:T(4,128)} %bitcast.55, bf16[512,1664]{0,1:T(8,128)(2,1)} %copy.35), kind=kOutput, calls=%fused_computation.15 | convolution fusion | flops 875233280 | bytes 8912896 | tf_op jit(solution)/shard_map/dot_general | solution.py:27
  317.3 0.2 reduce-scatter.9.cloned.1.call-start
  317.5 45.6 %all-gather.4.cloned.1.call-done = bf16[512,1664]{1,0:T(8,128)(2,1)} async-done(((bf16[32,1664]{1,0:T(8,128)(2,1)}), bf16[512,1664]{1,0:T(8,128)(2,1)}) %all-gather.4.cloned.1.call-update) | async-done | bytes 1703952 | tf_op jit(solution)/shard_map/all_gather | solution.py:49
  363.1 4.1 fusion.12
  367.2 3.8 fusion.3
  371.1 3.8 copy.42
  374.8 2.3 fusion.4
  377.1 3.8 copy.43
  380.9 2.3 convolution_convert_fusion
  383.1 37.6 %reduce-scatter.11.cloned.1.call-done = f32[32,512]{1,0:T(8,128)} async-done(((f32[512,512]{1,0:T(8,128)}), f32[32,512]{1,0:T(8,128)}) %reduce-scatter.11.cloned.1.call-update) | async-done | bytes 65552 | tf_op jit(solution)/shard_map/reduce_scatter | solution.py:75
  420.7 1.5 convert_element_type.58
  422.2 56.8 %reduce-scatter.9.cloned.1.call-done = f32[32,512]{1,0:T(8,128)} async-done(((f32[512,512]{1,0:T(8,128)}), f32[32,512]{1,0:T(8,128)}) %reduce-scatter.9.cloned.1.call-update) | async-done | bytes 65552 | tf_op jit(solution)/shard_map/reduce_scatter | solution.py:50
  479.0 1.5 convert_element_type.55
  (28 shorter events, 0.1 us)
Async XLA Ops:
  7.2 110.5 %reduce-scatter.15.cloned.1.call-start = ((), (), s32[]{:S(2)}) async-start(), calls=%async_computation.10 | async-start | bytes 3620864 | tf_op jit(solution)/shard_map/reduce_scatter | solution.py:55
  31.0 0.8 copy-start.7
  31.0 1.6 copy-start.4
  40.3 0.7 copy-start.12
  40.3 168.3 %reduce-scatter.13.cloned.1.call-start = ((), (), s32[]{:S(2)}) async-start(), calls=%async_computation.9 | async-start | bytes 7241728 | tf_op jit(solution)/shard_map/reduce_scatter | solution.py:38
  41.0 3.6 copy-start.13
  44.8 3.6 copy-start.11
  64.3 3.8 copy-start.5
  64.3 2.1 copy-start.2
  64.8 2.7 copy-start
  67.5 2.2 copy-start.3
  68.0 1.7 copy-start.1
  82.2 178.4 %all-gather.6.cloned.1.call-start = ((), (), s32[]{:S(2)}) async-start(), calls=%async_computation.6 | async-start | bytes 1810432 | tf_op jit(solution)/shard_map/all_gather | solution.py:63
  210.6 101.3 %all-gather.8.cloned.1.call-start = ((), (), s32[]{:S(2)}) async-start(), calls=%async_computation.7 | async-start | bytes 1810432 | tf_op jit(solution)/shard_map/all_gather | solution.py:64
  211.2 152.0 %all-gather.4.cloned.1.call-start = ((), (), s32[]{:S(2)}) async-start(), calls=%async_computation.4 | async-start | bytes 1810432 | tf_op jit(solution)/shard_map/all_gather | solution.py:49
  211.8 208.9 %reduce-scatter.11.cloned.1.call-start = ((), (), s32[]{:S(2)}) async-start(), calls=%async_computation.8 | async-start | bytes 1114112 | tf_op jit(solution)/shard_map/reduce_scatter | solution.py:75
  317.3 161.7 %reduce-scatter.9.cloned.1.call-start = ((), (), s32[]{:S(2)}) async-start(), calls=%async_computation.5 | async-start | bytes 1114112 | tf_op jit(solution)/shard_map/reduce_scatter | solution.py:50
  371.1 3.8 copy-start.6
  371.1 3.8 copy-start.9
  377.1 3.8 copy-start.8
  377.1 3.8 copy-start.10
Sparse Core Ops, SparseCore 0:
  40.4 77.1 reduce-scatter.14
  121.4 87.1 reduce-scatter.12
  211.9 48.6 all-gather.5
  263.2 48.6 all-gather.7
  314.5 48.6 all-gather.3
  365.7 54.9 reduce-scatter.10
  423.2 55.7 reduce-scatter.8
where the time goes:
time: 490 us; the launch traced here: 487 us
  waiting for transfers between devices  362 us (74%)
  blocking collectives  38.9 us (8%)
  local copies, waits for them, and re-layouts  34.9 us (7%)
  matrix products  27.9 us (6%)
  between operations  14.2 us (3%)
  other arithmetic  8.54 us (2%)
    reduce_scatter x1, waiting for transfers between devices, local(): lax.psum_scatter(jnp.concatenate([matmul(panel, w_gate), matmul(panel, w_...  91 us
    reduce_scatter x1, waiting for transfers between devices, local(): lax.psum_scatter(matmul(hidden, w_down), 'col', scatter_dimension=0, tile...  56.8 us
    all_gather x1, waiting for transfers between devices, local(): lax.all_gather(pre_gate, 'row', axis=0, tiled=True)  48.8 us
    all_gather x1, waiting for transfers between devices, local(): lax.all_gather(pre_up, 'row', axis=0, tiled=True)  46.2 us
    all_gather x1, waiting for transfers between devices, local(): hidden = lax.all_gather(hidden_part, 'row', axis=0, tiled=True)  45.6 us
    reduce_scatter x1, waiting for transfers between devices, local(): lax.psum_scatter(inner_last(gate_piece, w_gate) + inner_last(up_piece, w_...  37.6 us
    reduce_scatter x1, waiting for transfers between devices, local(): lax.psum_scatter(inner_last(grad_panel, w_down), 'row', scatter_dimension...  35.3 us
    unnamed x37, local copies, waits for them, and re-layouts  33.4 us
  transfers between devices with their start and end apart: 7, of which 7 were waited for; matrix products, arithmetic and copies ran while one was open for 11% of the time, Pallas kernels for 0%

commit v1 on v0

v1 whole, which is shorter than its diff:
```python
import jax
import jax.numpy as jnp
from jax import lax
from jax.experimental import pallas as pl
from jax.experimental.pallas import tpu as pltpu
from jax.sharding import PartitionSpec as P

F32 = jnp.float32
BF16 = jnp.bfloat16
BOTH = ("row", "col")


GRAY_A = (0, 1, 1, 0)
GRAY_B = (0, 0, 1, 1)
WIDE = 1664
SPLIT = 896
PART_A = WIDE + SPLIT
PART_B = WIDE + WIDE - SPLIT
LIMIT = 40 * 1024 * 1024


def code_of(y, x, core):
    along_x = 2 * GRAY_A[x] + GRAY_B[x]
    along_y = 2 * GRAY_A[y] + GRAY_B[y]
    return 4 * along_x + along_y if core == 0 else 4 * along_y + along_x


PLACE = {
    (code_of(y, x, core), core): y * 4 + x
    for y in range(4)
    for x in range(4)
    for core in range(2)
}


def flips(mask):
    pairs = []
    for row in range(16):
        for col in range(16):
            code = code_of(row // 4, row % 4, col % 2)
            pairs.append((row * 16 + col, PLACE[(code ^ mask, col % 2)] * 16 + col))
    return pairs


FLIPS = {mask: flips(mask) for mask in (1, 2, 3, 4, 8)}
CORES = [(i, i ^ 1) for i in range(16)]


def turn_by(shift):
    return [(i, (i + 2 * shift) % 16) for i in range(16)]


def swap_bits(j):
    return (j & 3) | ((j >> 2) & 1) << 3 | ((j >> 3) & 1) << 2


def send(x, mask):
    return lax.ppermute(x, BOTH, FLIPS[mask])


def tiles(start, stop):
    return [(at, min(at + 256, stop)) for at in range(start, stop, 256)]


def nn(left, right):
    return lax.dot_general(left, right, (((1,), (0,)), ((), ())), preferred_element_type=F32)


def nt(left, right):
    return lax.dot_general(left, right, (((1,), (1,)), ((), ())), preferred_element_type=F32)


def tn(left, right):
    return lax.dot_general(left, right, (((0,), (0,)), ((), ())), preferred_element_type=F32)


def run(kernel, outs, arrays, smem=0, scratch=(), flops=0):
    moved = sum(a.size * a.dtype.itemsize for a in arrays)
    shapes = [jax.ShapeDtypeStruct(shape, kind) for shape, kind in outs]
    moved += sum(s.size * s.dtype.itemsize for s in shapes)
    specs = [pl.BlockSpec(memory_space=pltpu.SMEM)] * smem
    specs += [pl.BlockSpec(memory_space=pltpu.VMEM)] * (len(arrays) - smem)
    return pl.pallas_call(
        kernel,
        out_shape=shapes,
        in_specs=specs,
        out_specs=[pl.BlockSpec(memory_space=pltpu.VMEM)] * len(shapes),
        scratch_shapes=list(scratch),
        compiler_params=pltpu.CompilerParams(vmem_limit_bytes=LIMIT),
        cost_estimate=pl.CostEstimate(flops=flops, bytes_accessed=moved, transcendentals=0),
    )(*arrays)


def arrange(index, panel, out):
    for part in range(2):
        for j in range(16):
            start = pl.multiple_of(index[j] * 32 + part * 16, 16)
            out[pl.ds(part * 256 + j * 16, 16), :] = panel[pl.ds(start, 16), :]


def scale_blocks(quant, scale, weight):
    block_rows, block_columns = scale.shape
    for r in range(block_rows):
        for c in range(block_columns):
            rows, columns = pl.ds(r * 128, 128), pl.ds(c * 128, 128)
            weight[rows, columns] = (quant[rows, columns].astype(F32) * scale[r, c]).astype(BF16)


def deal(product, at, stop, keep0, give0, keep1, give1):
    keep0[:, at:stop] = product[:128]
    give0[:, at:stop] = product[128:256].astype(BF16)
    keep1[:, at:stop] = product[256:384]
    give1[:, at:stop] = product[384:].astype(BF16)


def forward_kernel(index, scale, panel, quant, arranged, weight, *parts):
    arrange(index, panel, arranged)
    scale_blocks(quant, scale, weight)
    for at, stop in tiles(0, WIDE):
        deal(nn(arranged[...], weight[:, at:stop]), at, stop, *parts)


def parts_of(width):
    return [((128, width), F32), ((128, width), BF16)] * 2


def forward(index, scale, panel, quant):
    outs = [((512, 512), BF16), ((512, WIDE), BF16)] + parts_of(WIDE)
    return run(
        forward_kernel, outs, [index, scale, panel, quant], smem=2, flops=2 * 512 * 512 * WIDE
    )


def backward_kernel(index_a, index_b, scale, panel, quant, arranged_a, arranged_b, weight, *parts):
    arrange(index_a, panel, arranged_a)
    arrange(index_b, panel, arranged_b)
    scale_blocks(quant, scale, weight)
    for at, stop in tiles(0, SPLIT):
        deal(nt(arranged_a[...], weight[at:stop, :]), at, stop, *parts[:4])
    for at, stop in tiles(SPLIT, WIDE):
        deal(nt(arranged_b[...], weight[at:stop, :]), at - SPLIT, stop - SPLIT, *parts[4:])


def backward(index_a, index_b, scale, panel, quant):
    outs = [((512, 512), BF16)] * 2 + [((WIDE, 512), BF16)]
    outs += parts_of(SPLIT) + parts_of(WIDE - SPLIT)
    return run(
        backward_kernel,
        outs,
        [index_a, index_b, scale, panel, quant],
        smem=3,
        flops=2 * 512 * 512 * WIDE,
    )


def second_kernel(*refs):
    ins, (keep_a, give_a, keep_b, give_b) = refs[:8], refs[8:]
    for at, (held, came, keep, give) in (
        (0, (*ins[0:2], keep_a, give_a)),
        (WIDE, (*ins[2:4], keep_a, give_a)),
        (0, (*ins[4:6], keep_b, give_b)),
        (WIDE, (*ins[6:8], keep_b, give_b)),
    ):
        width = held.shape[1]
        keep[:, at : at + width] = held[:64] + came[:64].astype(F32)
        give[:, at : at + width] = held[64:] + came[64:].astype(F32)


def second(*arrays):
    outs = [((64, PART_A), F32)] * 2 + [((64, PART_B), F32)] * 2
    return run(second_kernel, outs, arrays)


def third_kernel(held_a, came_a, held_b, came_b, *outs):
    for j in range(4):
        rows = pl.ds(16 * j, 16)
        outs[j][:, :PART_A] = held_a[rows, :] + came_a[rows, :]
        outs[j][:, PART_A:] = held_b[rows, :] + came_b[rows, :]


def third(*arrays):
    return run(third_kernel, [((16, PART_A + PART_B), F32)] * 4, arrays)


def middle_kernel(held, came_1, came_2, came_3, out):
    def total(at, stop):
        return (held[:, at:stop] + came_1[:, at:stop]) + (came_2[:, at:stop] + came_3[:, at:stop])

    for at, stop in [(0, SPLIT), (SPLIT, WIDE)]:
        gate = total(at, stop)
        up = total(PART_A + at, PART_A + stop)
        offset = WIDE if at == 0 else PART_A + WIDE - SPLIT
        back = total(offset + at, offset + stop)
        sigmoid = 1.0 / (1.0 + jnp.exp(-gate))
        activated = gate * sigmoid
        out[:, offset + at : offset + stop] = (activated * up).astype(BF16)
        slope = sigmoid * (1.0 + gate * (1.0 - sigmoid))
        out[:, at:stop] = (back * up * slope).astype(BF16)
        out[:, PART_A + at : PART_A + stop] = (back * activated).astype(BF16)


def middle(*arrays):
    return run(middle_kernel, [((16, PART_A + PART_B), BF16)], arrays)[0]


def spread_kernel(*refs):
    ins, (out_a, out_b) = refs[:4], refs[4:]
    for j in range(4):
        out_a[pl.ds(16 * j, 16), :] = ins[j][:, :PART_A]
        out_b[pl.ds(16 * j, 16), :] = ins[j][:, PART_A:]


def spread(*arrays):
    return run(spread_kernel, [((64, PART_A), BF16), ((64, PART_B), BF16)], arrays)


def join_kernel(a, came_a, b, came_b, out_a, out_b):
    out_a[:64, :] = a[...]
    out_a[64:, :] = came_a[...]
    out_b[:64, :] = b[...]
    out_b[64:, :] = came_b[...]


def join(*arrays):
    return run(join_kernel, [((128, PART_A), BF16), ((128, PART_B), BF16)], arrays)


def project_kernel(index_a, index_b, a, came_a, b, came_b, gate, up, down, keep, give, sum_a, sum_b):
    for rows, left, right in ((0, a, b), (128, came_a, came_b)):
        at = pl.ds(rows, 128)
        sum_a[at, :512] = nn(left[:, WIDE:], down[:SPLIT, :])
        sum_b[at, :512] = nn(right[:, WIDE:], down[SPLIT:, :])
        sum_a[at, 512:] = nt(left[:, :WIDE], gate[...])
        sum_b[at, 512:] = nt(right[:, :WIDE], up[...])
    for k in range(16):
        out = keep if k < 8 else give
        from_a = pl.multiple_of(index_a[k] * 16, 16)
        from_b = pl.multiple_of(index_b[k] * 16, 16)
        out[pl.ds((k % 8) * 16, 16), :] = (
            sum_a[pl.ds(from_a, 16), :] + sum_b[pl.ds(from_b, 16), :]
        )


def project(*arrays):
    return run(
        project_kernel,
        [((128, 1024), F32)] * 2,
        arrays,
        smem=2,
        scratch=[pltpu.VMEM((256, 1024), F32)] * 2,
        flops=3 * 2 * 256 * 512 * WIDE,
    )


def chunk_kernel(keep_0, came_0, keep_1, came_1, own, *outs):
    for k in range(8):
        rows = pl.ds(16 * k, 16)
        out = own if k == 0 else outs[k - 1]
        out[:16, :] = (keep_0[rows, :] + came_0[rows, :]).astype(out.dtype)
        out[16:, :] = (keep_1[rows, :] + came_1[rows, :]).astype(out.dtype)


def chunk(*arrays):
    return run(chunk_kernel, [((32, 1024), F32)] + [((32, 1024), BF16)] * 7, arrays)


def finish_kernel(own, *refs):
    total = own[...]
    for came in refs[:7]:
        total = total + came[...].astype(F32)
    refs[7][...] = total[:, :512].astype(BF16)
    refs[8][...] = total[:, 512:].astype(BF16)


def finish(*arrays):
    return run(finish_kernel, [((32, 512), BF16)] * 2, arrays)


def wide_grad_kernel(panel, first, second, third, fourth, out):
    for at, stop in tiles(0, WIDE):
        pieces = [part[:, at:stop] for part in (first, second, third, fourth)]
        out[:, at:stop] = tn(panel[...], jnp.concatenate(pieces, axis=0)).astype(BF16)


def wide_grad(*arrays):
    return run(wide_grad_kernel, [((512, WIDE), BF16)], arrays, flops=2 * 512 * 512 * WIDE)[0]


def down_grad_kernel(panel_a, panel_b, *refs):
    out = refs[8]
    for panel, parts, offset, stop_at in (
        (panel_a, refs[:4], 0, SPLIT),
        (panel_b, refs[4:8], SPLIT, WIDE),
    ):
        for at, stop in tiles(offset, stop_at):
            shift = WIDE - offset
            pieces = [part[:, at + shift : stop + shift] for part in parts]
            out[at:stop, :] = tn(jnp.concatenate(pieces, axis=0), panel[...]).astype(BF16)


def down_gradient(*arrays):
    return run(down_grad_kernel, [((WIDE, 512), BF16)], arrays, flops=2 * 512 * 512 * WIDE)[0]


def local(tokens, gate_quant, gate_scale, up_quant, up_scale, down_quant, down_scale, out_grad):
    row = lax.axis_index("row")
    col = lax.axis_index("col")
    core = lax.rem(col, 2)
    depth = lax.div(col, 2)
    table = jnp.array(
        [[code_of(r // 4, r % 4, c) for c in range(2)] for r in range(16)], jnp.int32
    )
    code = table[row, core]
    blocks = jnp.arange(16, dtype=jnp.int32)

    def swapped(j):
        return (j & 3) | (((j >> 2) & 1) << 3) | (((j >> 3) & 1) << 2)

    index_a = blocks ^ code
    index_b = swapped(blocks) ^ code
    turn = lax.rem(depth + blocks % 8, 8) * 2
    home_a = (turn + jnp.where(blocks < 8, core, 1 - core)) ^ code
    home_b = swapped(home_a)

    panel = lax.all_gather(tokens, "col", axis=0, tiled=True)
    tokens_b, w_up, up_0, up_give_0, up_1, up_give_1 = forward(index_b, up_scale, panel, up_quant)
    up_came_0, up_came_1 = send(up_give_0, 4), send(up_give_1, 4)
    tokens_a, w_gate, gate_0, gate_give_0, gate_1, gate_give_1 = forward(
        index_a, gate_scale, panel, gate_quant
    )
    gate_came_0, gate_came_1 = send(gate_give_0, 8), send(gate_give_1, 8)

    grad_panel = lax.all_gather(out_grad, "col", axis=0, tiled=True)
    grads_a, grads_b, w_down, *back = backward(
        index_a, index_b, down_scale, grad_panel, down_quant
    )
    state = []
    for part, held in enumerate(
        ((gate_0, gate_came_0, up_0, up_came_0), (gate_1, gate_came_1, up_1, up_came_1))
    ):
        keep_a, give_a = back[2 * part : 2 * part + 2]
        keep_b, give_b = back[4 + 2 * part : 6 + 2 * part]
        state.append(
            (*held[:2], keep_a, send(give_a, 8), *held[2:], keep_b, send(give_b, 4))
        )
    for part in range(2):
        keep_a, give_a, keep_b, give_b = second(*state[part])
        state[part] = (keep_a, send(give_a, 4), keep_b, send(give_b, 8))
    for part in range(2):
        held, *give = third(*state[part])
        state[part] = (held, *(send(give[j - 1], j) for j in (1, 2, 3)))
    for part in range(2):
        own = middle(*state[part])
        state[part] = (own, *(send(own, j) for j in (1, 2, 3)))
    for part in range(2):
        a, b = spread(*state[part])
        state[part] = (a, send(a, 4), b, send(b, 8))
    for part in range(2):
        a, b = join(*state[part])
        state[part] = (a, send(a, 8), b, send(b, 4))
    ends = []
    for part in range(2):
        keep, give = project(home_a, home_b, *state[part], w_gate, w_up, w_down)
        ends += [keep, lax.ppermute(give, "col", CORES)]
    own, *sent = chunk(*ends)
    output, input_grad = finish(
        own, *(lax.ppermute(sent[k - 1], "col", turn_by(k)) for k in range(1, 8))
    )
    all_a = [*state[0][:2], *state[1][:2]]
    all_b = [*state[0][2:], *state[1][2:]]
    gate_grad = wide_grad(tokens_a, *all_a)
    up_grad = wide_grad(tokens_b, *all_b)
    down_grad = down_gradient(grads_a, grads_b, *all_a, *all_b)
    return (output, input_grad, gate_grad, up_grad, down_grad)


def solution(mesh):
    placed = (
        P("col", "row"),
        P("row", "col"),
        P("row", "col"),
        P("row", "col"),
        P("row", "col"),
        P("col", "row"),
        P("col", "row"),
        P("col", "row"),
    )
    return jax.shard_map(
        local,
        mesh=mesh,
        in_specs=placed,
        out_specs=(
            P("col", "row"),
            P("col", "row"),
            P("row", "col"),
            P("row", "col"),
            P("col", "row"),
        ),
        check_vma=False,
    )
```

time: 490 us -> 183 us (0.37)
  waiting for transfers between devices: 362 us -> 44.1 us
  starting transfers between devices: 0.46 us -> 48 us
  Pallas kernels: 0 us -> 34.3 us
  matrix products: 27.9 us -> 0 us
  local copies, waits for them, and re-layouts: 34.9 us -> 15.1 us
  between operations: 14.2 us -> 0.85 us
  other arithmetic: 8.54 us -> 1.31 us
    reduce_scatter x4 -> x0, waiting for transfers between devices: 221 us -> none  [the longest x1 91 us: local(): lax.psum_scatter(jnp.concatenate([matmul(panel, w_gate), matmul(panel, w_...]
    all_gather x3 -> x0, waiting for transfers between devices: 141 us -> none  [the longest x1 48.8 us: local(): lax.all_gather(pre_gate, 'row', axis=0, tiled=True)]
    ppermute x0 -> x41, starting transfers between devices: none -> 48 us  [the longest x32 31.5 us: send(): return lax.ppermute(x, BOTH, FLIPS[mask])]
    ppermute x0 -> x41, waiting for transfers between devices: none -> 44.1 us  [the longest x32 41 us: send(): return lax.ppermute(x, BOTH, FLIPS[mask])]
    pallas_call x0 -> x20, Pallas kernels: none -> 34.3 us  [run(): pl.pallas_call(kernel, out_shape=shapes, in_specs=specs, out_specs=[pl.Bl...]
    dot_general x9 -> x0, matrix products: 27.9 us -> none  [the longest x3 13.3 us: inner_last(): lax.dot_general(left, right, (((1,), (1,)), ((), ())), preferred_element_...]
    unnamed x37 -> x59, local copies, waits for them, and re-layouts: 33.4 us -> 13.9 us
    all_gather x1, blocking collectives: 15.9 us -> 23 us  [local(): panel = lax.all_gather(tokens, 'col', axis=0, tiled=True)]
  transfers between devices with their start and end apart: 7 -> 41, of which waited for: 7 -> 17; matrix products, arithmetic and copies ran while one was open for 11% -> 0% of each run, Pallas kernels for 0% -> 17%
where the time goes in v1:
time: 183 us
  starting transfers between devices  48 us (26%)
  waiting for transfers between devices  44.1 us (24%)
  blocking collectives  39 us (21%)
  Pallas kernels  34.3 us (19%)
  local copies, waits for them, and re-layouts  15.1 us (8%)
    ppermute x32, waiting for transfers between devices, send(): return lax.ppermute(x, BOTH, FLIPS[mask])  41 us
    pallas_call x20, Pallas kernels, run(): pl.pallas_call(kernel, out_shape=shapes, in_specs=specs, out_specs=[pl.Bl...  34.3 us
    ppermute x32, starting transfers between devices, send(): return lax.ppermute(x, BOTH, FLIPS[mask])  31.5 us
    all_gather x1, blocking collectives, local(): panel = lax.all_gather(tokens, 'col', axis=0, tiled=True)  23 us
    all_gather x1, blocking collectives, local(): grad_panel = lax.all_gather(out_grad, 'col', axis=0, tiled=True)  16 us
    unnamed x59, local copies, waits for them, and re-layouts  13.9 us
    ppermute x7, starting transfers between devices, local(): lax.ppermute(sent[k - 1], 'col', turn_by(k))  11.9 us
    ppermute x2, starting transfers between devices, local(): ends += [keep, lax.ppermute(give, 'col', CORES)]  4.52 us
  transfers between devices with their start and end apart: 41, of which 17 were waited for; matrix products, arithmetic and copies ran while one was open for 0% of the time, Pallas kernels for 17%

profile of v1, /device:TPU:1, one launch (start us, length us, event | category | flops | bytes accessed | tf_op | source)
XLA Modules:
  0.0 182.7 jit_solution(9801638482444047844)
XLA Ops:
  0.6 1.3 dynamic_slice.3
  2.6 23.0 %all_gather.6.panel = bf16[512,512]{1,0:T(8,128)(2,1)S(1)} all-gather(bf16[32,512]{1,0:T(8,128)(2,1)} %param.9), channel_id=1, replica_groups=mesh['row'=16,'col'=16] {'col'}, dimensions={0}, use_global_device_ids=true | all-gather | bytes 557056 | tf_op jit(solution)/shard_map/all_gather | solution.py:325
  25.6 1.5 copy-done.18
  27.7 2.6 %shard_map.130 = (bf16[512,512]{1,0:T(8,128)(2,1)S(1)}, bf16[512,1664]{1,0:T(8,128)(2,1)S(1)}, f32[128,1664]{1,0:T(8,128)S(1)}, bf16[128,1664]{1,0:T(8,128)(2,1)...) custom-call(s32[16]{0:T(128)S(1)} %get-tuple-element.129.index_b.index, f32[4,13]{1,0:T(4,128)S(1)} %copy-done.25, ...), custom_call_target="tpu_custom_call" | custom-call | flops 872415232 | bytes 7012624 | tf_op jit(solution)/shard_map/pallas_call | solution.py:83
  32.8 2.7 %collective-permute-start.2 = (bf16[128,1664]{1,0:T(8,128)(2,1)}, bf16[128,1664]{1,0:T(8,128)(2,1)}, u32[]{:S(2)}, u32[]{:S(2)}) collective-permute-start(bf16[128,1664]{1,0:T(8,128)(2,1)} %get-tuple-element.71), channel_id=1, source_target_pairs={{0,48},{1,193},{2,50},{3,195},{4,52},{5,197},{6,54},{7,199},{8,56}... | collective-permute-start | bytes 1277960 | tf_op jit(solution)/shard_map/ppermute | solution.py:58
  35.5 2.6 %shard_map.128 = (bf16[512,512]{1,0:T(8,128)(2,1)S(1)}, bf16[512,1664]{1,0:T(8,128)(2,1)S(1)}, f32[128,1664]{1,0:T(8,128)S(1)}, bf16[128,1664]{1,0:T(8,128)(2,1)...) custom-call(s32[16]{0:T(128)S(1)} %get-tuple-element.130.index.index_a, f32[4,13]{1,0:T(4,128)S(1)} %copy-done.26, ...), custom_call_target="tpu_custom_call" | custom-call | flops 872415232 | bytes 7012624 | tf_op jit(solution)/shard_map/pallas_call | solution.py:83
  41.6 16.0 %all_gather.7.panel = bf16[512,512]{1,0:T(8,128)(2,1)S(1)} all-gather(bf16[32,512]{1,0:T(8,128)(2,1)S(1)} %copy-done.27), channel_id=1, replica_groups=mesh['row'=16,'col'=16] {'col'}, dimensions={0}, use_global_device_ids=true | all-gather | bytes 557056 | tf_op jit(solution)/shard_map/all_gather | solution.py:333
  57.5 1.5 copy-done.20
  59.0 1.9 %shard_map.129 = (bf16[512,512]{1,0:T(8,128)(2,1)S(1)}, bf16[512,512]{1,0:T(8,128)(2,1)S(1)}, bf16[1664,512]{1,0:T(8,128)(2,1)S(1)}, f32[128,896]{1,0:T(8,128)S(...) custom-call(s32[16]{0:T(128)S(1)} %get-tuple-element.130.index.index, ...), custom_call_target="tpu_custom_call" | custom-call | flops 872415232 | bytes 7536976 | tf_op jit(solution)/shard_map/pallas_call | solution.py:83
  60.9 1.2 copy-done
  63.7 2.7 %collective-permute-start.3 = (bf16[128,768]{1,0:T(8,128)(2,1)S(1)}, bf16[128,768]{1,0:T(8,128)(2,1)S(1)}, u32[]{:S(2)}, u32[]{:S(2)}) collective-permute-start(bf16[128,768]{1,0:T(8,128)(2,1)S(1)} %get-tuple-element.73), channel_id=1, source_target_pairs={{0,48},{1,193},{2,50},{3,195},{4,52},{5,197},{6,54},{7,199},{8,56}... | collective-permute-start | bytes 589832 | tf_op jit(solution)/shard_map/ppermute | solution.py:58
  67.2 2.6 %collective-permute-done.3.refs_7_ = bf16[128,768]{1,0:T(8,128)(2,1)S(1)} collective-permute-done((bf16[128,768]{1,0:T(8,128)(2,1)S(1)}, bf16[128,768]{1,0:T(8,128)(2,1)S(1)}, u32[]{:S(2)}, u32[]{:S(2)}) %collective-permute-start.3) | collective-permute-done | bytes 196640 | tf_op jit(solution)/shard_map/ppermute | solution.py:58
  69.9 1.7 collective-permute-done.1.refs_3_
  73.4 1.5 shard_map.131
  75.9 1.7 collective-permute-done.20.refs_7_
  77.6 1.9 %collective-permute-done.18.refs_3_ = bf16[128,896]{1,0:T(8,128)(2,1)S(1)} collective-permute-done((bf16[128,896]{1,0:T(8,128)(2,1)S(1)}, bf16[128,896]{1,0:T(8,128)(2,1)S(1)}, u32[]{:S(2)}, u32[]{:S(2)}) %collective-permute-start.18) | collective-permute-done | bytes 229408 | tf_op jit(solution)/shard_map/ppermute | solution.py:58
  79.8 2.8 %collective-permute-start.21 = (f32[64,2560]{1,0:T(8,128)S(1)}, f32[64,2560]{1,0:T(8,128)S(1)}, u32[]{:S(2)}, u32[]{:S(2)}) collective-permute-start(f32[64,2560]{1,0:T(8,128)S(1)} %get-tuple-element.100), channel_id=1, source_target_pairs={{0,48},{1,193},{2,50},{3,195},{4,52},{5,197},{6,54},{7,199},{8,56}... | collective-permute-start | bytes 1966088 | tf_op jit(solution)/shard_map/ppermute | solution.py:58
  82.5 4.5 %collective-permute-done.5.came_b = f32[64,2432]{1,0:T(8,128)S(1)} collective-permute-done((f32[64,2432]{1,0:T(8,128)S(1)}, f32[64,2432]{1,0:T(8,128)S(1)}, u32[]{:S(2)}, u32[]{:S(2)}) %collective-permute-start.5) | collective-permute-done | bytes 622624 | tf_op jit(solution)/shard_map/ppermute | solution.py:58
  87.2 1.6 collective-permute-start.6
  88.8 2.3 %collective-permute-start.8 = (f32[16,4992]{1,0:T(8,128)S(1)}, f32[16,4992]{1,0:T(8,128)S(1)}, u32[]{:S(2)}, u32[]{:S(2)}) collective-permute-start(f32[16,4992]{1,0:T(8,128)S(1)} %get-tuple-element.81), channel_id=1, source_target_pairs={{0,128},{1,33},{2,130},{3,35},{4,132},{5,37},{6,134},{7,39},{8,136... | collective-permute-start | bytes 958472 | tf_op jit(solution)/shard_map/ppermute | solution.py:58
  91.1 2.6 %collective-permute-done.22.came_b = f32[64,2432]{1,0:T(8,128)S(1)} collective-permute-done((f32[64,2432]{1,0:T(8,128)S(1)}, f32[64,2432]{1,0:T(8,128)S(1)}, u32[]{:S(2)}, u32[]{:S(2)}) %collective-permute-start.22) | collective-permute-done | bytes 622624 | tf_op jit(solution)/shard_map/ppermute | solution.py:58
  93.8 1.6 collective-permute-start.23
  95.5 2.6 %collective-permute-done.6.came_1 = f32[16,4992]{1,0:T(8,128)S(1)} collective-permute-done((f32[16,4992]{1,0:T(8,128)S(1)}, f32[16,4992]{1,0:T(8,128)S(1)}, u32[]{:S(2)}, u32[]{:S(2)}) %collective-permute-start.6) | collective-permute-done | bytes 319520 | tf_op jit(solution)/shard_map/ppermute | solution.py:58
  98.4 4.7 %collective-permute-done.8.came_3 = f32[16,4992]{1,0:T(8,128)S(1)} collective-permute-done((f32[16,4992]{1,0:T(8,128)S(1)}, f32[16,4992]{1,0:T(8,128)S(1)}, u32[]{:S(2)}, u32[]{:S(2)}) %collective-permute-start.8) | collective-permute-done | bytes 319520 | tf_op jit(solution)/shard_map/ppermute | solution.py:58
  104.1 1.7 collective-permute-start.10
  106.5 3.4 %collective-permute-done.25.came_3 = f32[16,4992]{1,0:T(8,128)S(1)} collective-permute-done((f32[16,4992]{1,0:T(8,128)S(1)}, f32[16,4992]{1,0:T(8,128)S(1)}, u32[]{:S(2)}, u32[]{:S(2)}) %collective-permute-start.25) | collective-permute-done | bytes 319520 | tf_op jit(solution)/shard_map/ppermute | solution.py:58
  110.9 2.0 %collective-permute-start.27 = (bf16[16,4992]{1,0:T(8,128)(2,1)S(1)}, bf16[16,4992]{1,0:T(8,128)(2,1)S(1)}, u32[]{:S(2)}, u32[]{:S(2)}) collective-permute-start(bf16[16,4992]{1,0:T(8,128)(2,1)S(1)} %shard_map.139.refs_0_), channel_id=1, source_target_pairs={{0,64},{1,17},{2,66},{3,19},{4,68},{5,21},{6,70},{7,23},{8,72},{9,... | collective-permute-start | bytes 479240 | tf_op jit(solution)/shard_map/ppermute | solution.py:58
  113.9 2.1 %collective-permute-start.12 = (bf16[64,2560]{1,0:T(8,128)(2,1)S(1)}, bf16[64,2560]{1,0:T(8,128)(2,1)S(1)}, u32[]{:S(2)}, u32[]{:S(2)}) collective-permute-start(bf16[64,2560]{1,0:T(8,128)(2,1)S(1)} %get-tuple-element.82.a), channel_id=1, source_target_pairs={{0,48},{1,193},{2,50},{3,195},{4,52},{5,197},{6,54},{7,199},{8,56}... | collective-permute-start | bytes 983048 | tf_op jit(solution)/shard_map/ppermute | solution.py:58
  116.0 1.5 collective-permute-done.27.refs_2_
  118.6 1.3 collective-permute-start.29
  119.9 5.1 %collective-permute-done.13.came_b = bf16[64,2432]{1,0:T(8,128)(2,1)S(1)} collective-permute-done((bf16[64,2432]{1,0:T(8,128)(2,1)S(1)}, bf16[64,2432]{1,0:T(8,128)(2,1)S(1)}, u32[]{:S(2)}, u32[]{:S(2)}) %collective-permute-start.13) | collective-permute-done | bytes 311328 | tf_op jit(solution)/shard_map/ppermute | solution.py:58
  125.4 1.1 shard_map.135
  126.5 1.4 collective-permute-start.14
  129.4 1.2 shard_map.141
  130.6 1.1 collective-permute-start.31
  133.0 5.9 %collective-permute-done.15.came_b.second.refs_5_ = bf16[128,2432]{1,0:T(8,128)(2,1)} collective-permute-done((bf16[128,2432]{1,0:T(8,128)(2,1)}, bf16[128,2432]{1,0:T(8,128)(2,1)}, u32[]{:S(2)}, u32[]{:S(2)}) %collective-permute-start.15) | collective-permute-done | bytes 622624 | tf_op jit(solution)/shard_map/ppermute | solution.py:58
  138.8 1.5 copy-done.1
  140.3 4.6 %shard_map.136 = (f32[128,1024]{1,0:T(8,128)S(1)}, f32[128,1024]{1,0:T(8,128)S(1)}) custom-call(s32[16]{0:T(128)S(1)} %get-tuple-element.128.index_a, s32[16]{0:T(128)S(1)} %get-tuple-element.127.index_b, bf16[128,2560]{1,0:T(8,128)(2,1)} %get-tuple-element.84.a.first.refs_0_, bf16[128,2560]{1,0:T(8,128)(2,1)} %collective-permute-done.14.came_a.second.refs_1_, ...), custom_call_target="tpu_custom_call" | custom-call | flops 1308622848 | bytes 8716416 | tf_op jit(solution)/shard_map/pallas_call | solution.py:83
  144.9 3.9 %collective-permute-start.16 = (f32[128,1024]{1,0:T(8,128)S(1)}, f32[128,1024]{1,0:T(8,128)S(1)}, u32[]{:S(2)}, u32[]{:S(2)}) collective-permute-start(f32[128,1024]{1,0:T(8,128)S(1)} %get-tuple-element.90), channel_id=1, source_target_pairs={{0,1},{1,0},{2,3},{3,2},{4,5},{5,4},{6,7},{7,6},{8,9},{9,8},{10,11... | collective-permute-start | bytes 1572872 | tf_op jit(solution)/shard_map/ppermute | solution.py:364
  148.8 4.6 %shard_map.142 = (f32[128,1024]{1,0:T(8,128)S(1)}, f32[128,1024]{1,0:T(8,128)S(1)}) custom-call(s32[16]{0:T(128)S(1)} %get-tuple-element.128.index_a, s32[16]{0:T(128)S(1)} %get-tuple-element.127.index_b, bf16[128,2560]{1,0:T(8,128)(2,1)} %get-tuple-element.109.a.third.refs_2_, bf16[128,2560]{1,0:T(8,128)(2,1)} %collective-permute-done.31.came_a.fourth.refs_3_, ...), custom_call_target="tpu_custom_call" | custom-call | flops 1308622848 | bytes 8716416 | tf_op jit(solution)/shard_map/pallas_call | solution.py:83
  154.0 4.0 %shard_map.146 = bf16[512,1664]{1,0:T(8,128)(2,1)} custom-call(bf16[512,512]{1,0:T(8,128)(2,1)S(1)} %copy-done.13, bf16[128,2432]{1,0:T(8,128)(2,1)} %get-tuple-element.85.b.first.refs_4_, bf16[128,2432]{1,0:T(8,128)(2,1)} %collective-permute-done.15.came_b.second.refs_5_, bf16[128,2432]{1,0:T(8,128)(2,1)} %get-tuple-element.110.b.third.refs_6_, ...), custom_call_target="tpu_custom_call" | custom-call | flops 872415232 | bytes 4718592 | tf_op jit(solution)/shard_map/pallas_call | solution.py:83
  159.2 4.1 %shard_map.145 = bf16[512,1664]{1,0:T(8,128)(2,1)} custom-call(bf16[512,512]{1,0:T(8,128)(2,1)S(1)} %copy-done.11, bf16[128,2560]{1,0:T(8,128)(2,1)} %get-tuple-element.84.a.first.refs_0_, bf16[128,2560]{1,0:T(8,128)(2,1)} %collective-permute-done.14.came_a.second.refs_1_, bf16[128,2560]{1,0:T(8,128)(2,1)} %get-tuple-element.109.a.third.refs_2_, ...), custom_call_target="tpu_custom_call" | custom-call | flops 872415232 | bytes 4849664 | tf_op jit(solution)/shard_map/pallas_call | solution.py:83
  163.3 2.1 %collective-permute-start.36 = (bf16[32,1024]{1,0:T(8,128)(2,1)S(1)}, bf16[32,1024]{1,0:T(8,128)(2,1)S(1)}, u32[]{:S(2)}, u32[]{:S(2)}) collective-permute-start(bf16[32,1024]{1,0:T(8,128)(2,1)S(1)} %get-tuple-element.116), channel_id=1, source_target_pairs={{0,6},{1,7},{2,8},{3,9},{4,10},{5,11},{6,12},{7,13},{8,14},{9,15},... | collective-permute-start | bytes 196616 | tf_op jit(solution)/shard_map/ppermute | solution.py:367
  165.4 3.3 %collective-permute-start.37 = (bf16[32,1024]{1,0:T(8,128)(2,1)S(1)}, bf16[32,1024]{1,0:T(8,128)(2,1)S(1)}, u32[]{:S(2)}, u32[]{:S(2)}) collective-permute-start(bf16[32,1024]{1,0:T(8,128)(2,1)S(1)} %get-tuple-element.117), channel_id=1, source_target_pairs={{0,8},{1,9},{2,10},{3,11},{4,12},{5,13},{6,14},{7,15},{8,0},{9,1},... | collective-permute-start | bytes 196616 | tf_op jit(solution)/shard_map/ppermute | solution.py:367
  168.8 2.3 %collective-permute-start.38 = (bf16[32,1024]{1,0:T(8,128)(2,1)S(1)}, bf16[32,1024]{1,0:T(8,128)(2,1)S(1)}, u32[]{:S(2)}, u32[]{:S(2)}) collective-permute-start(bf16[32,1024]{1,0:T(8,128)(2,1)S(1)} %get-tuple-element.118), channel_id=1, source_target_pairs={{0,10},{1,11},{2,12},{3,13},{4,14},{5,15},{6,0},{7,1},{8,2},{9,3},... | collective-permute-start | bytes 196616 | tf_op jit(solution)/shard_map/ppermute | solution.py:367
  171.0 2.4 %collective-permute-start.39 = (bf16[32,1024]{1,0:T(8,128)(2,1)S(1)}, bf16[32,1024]{1,0:T(8,128)(2,1)S(1)}, u32[]{:S(2)}, u32[]{:S(2)}) collective-permute-start(bf16[32,1024]{1,0:T(8,128)(2,1)S(1)} %get-tuple-element.119), channel_id=1, source_target_pairs={{0,12},{1,13},{2,14},{3,15},{4,0},{5,1},{6,2},{7,3},{8,4},{9,5},{1... | collective-permute-start | bytes 196616 | tf_op jit(solution)/shard_map/ppermute | solution.py:367
  174.1 4.7 %shard_map.147 = bf16[1664,512]{1,0:T(8,128)(2,1)} custom-call(bf16[512,512]{1,0:T(8,128)(2,1)S(1)} %copy-done.15, bf16[512,512]{1,0:T(8,128)(2,1)S(1)} %copy-done.17, bf16[128,2560]{1,0:T(8,128)(2,1)} %get-tuple-element.84.a.first.refs_0_, bf16[128,2560]{1,0:T(8,128)(2,1)} %collective-permute-done.14.came_a.second.refs_1_, ...), custom_call_target="tpu_custom_call" | custom-call | flops 872415232 | bytes 7864320 | tf_op jit(solution)/shard_map/pallas_call | solution.py:83
  178.9 3.1 %collective-permute-done.39.refs_5_ = bf16[32,1024]{1,0:T(8,128)(2,1)S(1)} collective-permute-done((bf16[32,1024]{1,0:T(8,128)(2,1)S(1)}, bf16[32,1024]{1,0:T(8,128)(2,1)S(1)}, u32[]{:S(2)}, u32[]{:S(2)}) %collective-permute-start.39) | collective-permute-done | bytes 65568 | tf_op jit(solution)/shard_map/ppermute | solution.py:367
  (118 shorter events, 24.6 us)
Async XLA Ops:
  32.8 8.8 %copy-start.27 = (bf16[32,512]{1,0:T(8,128)(2,1)S(1)}, bf16[32,512]{1,0:T(8,128)(2,1)}, u32[]{:S(2)}) copy-start(bf16[32,512]{1,0:T(8,128)(2,1)} %param.16) | copy-start | bytes 98308
  32.8 39.8 %collective-permute-start.2 = (bf16[128,1664]{1,0:T(8,128)(2,1)}, bf16[128,1664]{1,0:T(8,128)(2,1)}, u32[]{:S(2)}, u32[]{:S(2)}) collective-permute-start(bf16[128,1664]{1,0:T(8,128)(2,1)} %get-tuple-element.71), channel_id=1, source_target_pairs={{0,48},{1,193},{2,50},{3,195},{4,52},{5,197},{6,54},{7,199},{8,56}... | collective-permute-start | bytes 1277960 | tf_op jit(solution)/shard_map/ppermute | solution.py:58
  41.4 31.9 %collective-permute-start = (bf16[128,1664]{1,0:T(8,128)(2,1)}, bf16[128,1664]{1,0:T(8,128)(2,1)}, u32[]{:S(2)}, u32[]{:S(2)}) collective-permute-start(bf16[128,1664]{1,0:T(8,128)(2,1)} %get-tuple-element.67), channel_id=1, source_target_pairs={{0,16},{1,65},{2,18},{3,67},{4,20},{5,69},{6,22},{7,71},{8,24},{9,... | collective-permute-start | bytes 1277960 | tf_op jit(solution)/shard_map/ppermute | solution.py:58
  59.0 10.8 %copy-start.24 = (bf16[128,1664]{1,0:T(8,128)(2,1)S(1)}, bf16[128,1664]{1,0:T(8,128)(2,1)}, u32[]{:S(2)}) copy-start(bf16[128,1664]{1,0:T(8,128)(2,1)} %copy-done.23) | copy-start | bytes 1277956
  59.0 14.4 %copy-start.7 = (f32[128,1664]{1,0:T(8,128)S(1)}, f32[128,1664]{1,0:T(8,128)}, u32[]{:S(2)}) copy-start(f32[128,1664]{1,0:T(8,128)} %copy-done.6) | copy-start | bytes 2555908
  59.0 14.4 %copy-start.9 = (f32[128,1664]{1,0:T(8,128)S(1)}, f32[128,1664]{1,0:T(8,128)}, u32[]{:S(2)}) copy-start(f32[128,1664]{1,0:T(8,128)} %copy-done.8) | copy-start | bytes 2555908
  63.7 6.1 %collective-permute-start.3 = (bf16[128,768]{1,0:T(8,128)(2,1)S(1)}, bf16[128,768]{1,0:T(8,128)(2,1)S(1)}, u32[]{:S(2)}, u32[]{:S(2)}) collective-permute-start(bf16[128,768]{1,0:T(8,128)(2,1)S(1)} %get-tuple-element.73), channel_id=1, source_target_pairs={{0,48},{1,193},{2,50},{3,195},{4,52},{5,197},{6,54},{7,199},{8,56}... | collective-permute-start | bytes 589832 | tf_op jit(solution)/shard_map/ppermute | solution.py:58
  66.4 5.2 %collective-permute-start.1 = (bf16[128,896]{1,0:T(8,128)(2,1)S(1)}, bf16[128,896]{1,0:T(8,128)(2,1)S(1)}, u32[]{:S(2)}, u32[]{:S(2)}) collective-permute-start(bf16[128,896]{1,0:T(8,128)(2,1)S(1)} %get-tuple-element.69), channel_id=1, source_target_pairs={{0,16},{1,65},{2,18},{3,67},{4,20},{5,69},{6,22},{7,71},{8,24},{9,... | collective-permute-start | bytes 688136 | tf_op jit(solution)/shard_map/ppermute | solution.py:58
  66.4 13.1 %collective-permute-start.19 = (bf16[128,1664]{1,0:T(8,128)(2,1)S(1)}, bf16[128,1664]{1,0:T(8,128)(2,1)S(1)}, u32[]{:S(2)}, u32[]{:S(2)}) collective-permute-start(bf16[128,1664]{1,0:T(8,128)(2,1)S(1)} %copy-done.22), channel_id=1, source_target_pairs={{0,48},{1,193},{2,50},{3,195},{4,52},{5,197},{6,54},{7,199},{8,56}... | collective-permute-start | bytes 1277960 | tf_op jit(solution)/shard_map/ppermute | solution.py:58
  69.8 9.7 %collective-permute-start.17 = (bf16[128,1664]{1,0:T(8,128)(2,1)S(1)}, bf16[128,1664]{1,0:T(8,128)(2,1)S(1)}, u32[]{:S(2)}, u32[]{:S(2)}) collective-permute-start(bf16[128,1664]{1,0:T(8,128)(2,1)S(1)} %copy-done.24), channel_id=1, source_target_pairs={{0,16},{1,65},{2,18},{3,67},{4,20},{5,69},{6,22},{7,71},{8,24},{9,... | collective-permute-start | bytes 1277960 | tf_op jit(solution)/shard_map/ppermute | solution.py:58
  71.6 6.0 %collective-permute-start.20 = (bf16[128,768]{1,0:T(8,128)(2,1)S(1)}, bf16[128,768]{1,0:T(8,128)(2,1)S(1)}, u32[]{:S(2)}, u32[]{:S(2)}) collective-permute-start(bf16[128,768]{1,0:T(8,128)(2,1)S(1)} %get-tuple-element.98), channel_id=1, source_target_pairs={{0,48},{1,193},{2,50},{3,195},{4,52},{5,197},{6,54},{7,199},{8,56}... | collective-permute-start | bytes 589832 | tf_op jit(solution)/shard_map/ppermute | solution.py:58
  72.6 7.0 %collective-permute-start.18 = (bf16[128,896]{1,0:T(8,128)(2,1)S(1)}, bf16[128,896]{1,0:T(8,128)(2,1)S(1)}, u32[]{:S(2)}, u32[]{:S(2)}) collective-permute-start(bf16[128,896]{1,0:T(8,128)(2,1)S(1)} %get-tuple-element.94), channel_id=1, source_target_pairs={{0,16},{1,65},{2,18},{3,67},{4,20},{5,69},{6,22},{7,71},{8,24},{9,... | collective-permute-start | bytes 688136 | tf_op jit(solution)/shard_map/ppermute | solution.py:58
  74.8 12.2 %collective-permute-start.4 = (f32[64,2560]{1,0:T(8,128)S(1)}, f32[64,2560]{1,0:T(8,128)S(1)}, u32[]{:S(2)}, u32[]{:S(2)}) collective-permute-start(f32[64,2560]{1,0:T(8,128)S(1)} %get-tuple-element.75), channel_id=1, source_target_pairs={{0,48},{1,193},{2,50},{3,195},{4,52},{5,197},{6,54},{7,199},{8,56}... | collective-permute-start | bytes 1966088 | tf_op jit(solution)/shard_map/ppermute | solution.py:58
  77.6 9.4 %collective-permute-start.5 = (f32[64,2432]{1,0:T(8,128)S(1)}, f32[64,2432]{1,0:T(8,128)S(1)}, u32[]{:S(2)}, u32[]{:S(2)}) collective-permute-start(f32[64,2432]{1,0:T(8,128)S(1)} %get-tuple-element.77), channel_id=1, source_target_pairs={{0,16},{1,65},{2,18},{3,67},{4,20},{5,69},{6,22},{7,71},{8,24},{9,... | collective-permute-start | bytes 1867784 | tf_op jit(solution)/shard_map/ppermute | solution.py:58
  79.8 13.9 %collective-permute-start.21 = (f32[64,2560]{1,0:T(8,128)S(1)}, f32[64,2560]{1,0:T(8,128)S(1)}, u32[]{:S(2)}, u32[]{:S(2)}) collective-permute-start(f32[64,2560]{1,0:T(8,128)S(1)} %get-tuple-element.100), channel_id=1, source_target_pairs={{0,48},{1,193},{2,50},{3,195},{4,52},{5,197},{6,54},{7,199},{8,56}... | collective-permute-start | bytes 1966088 | tf_op jit(solution)/shard_map/ppermute | solution.py:58
  82.5 11.2 %collective-permute-start.22 = (f32[64,2432]{1,0:T(8,128)S(1)}, f32[64,2432]{1,0:T(8,128)S(1)}, u32[]{:S(2)}, u32[]{:S(2)}) collective-permute-start(f32[64,2432]{1,0:T(8,128)S(1)} %get-tuple-element.102), channel_id=1, source_target_pairs={{0,16},{1,65},{2,18},{3,67},{4,20},{5,69},{6,22},{7,71},{8,24},{9,... | collective-permute-start | bytes 1867784 | tf_op jit(solution)/shard_map/ppermute | solution.py:58
  87.2 10.9 %collective-permute-start.6 = (f32[16,4992]{1,0:T(8,128)S(1)}, f32[16,4992]{1,0:T(8,128)S(1)}, u32[]{:S(2)}, u32[]{:S(2)}) collective-permute-start(f32[16,4992]{1,0:T(8,128)S(1)} %get-tuple-element.79), channel_id=1, source_target_pairs={{0,192},{1,49},{2,194},{3,51},{4,196},{5,53},{6,198},{7,55},{8,200... | collective-permute-start | bytes 958472 | tf_op jit(solution)/shard_map/ppermute | solution.py:58
  88.8 9.6 %collective-permute-start.7 = (f32[16,4992]{1,0:T(8,128)S(1)}, f32[16,4992]{1,0:T(8,128)S(1)}, u32[]{:S(2)}, u32[]{:S(2)}) collective-permute-start(f32[16,4992]{1,0:T(8,128)S(1)} %get-tuple-element.80), channel_id=1, source_target_pairs={{0,64},{1,17},{2,66},{3,19},{4,68},{5,21},{6,70},{7,23},{8,72},{9,... | collective-permute-start | bytes 958472 | tf_op jit(solution)/shard_map/ppermute | solution.py:58
  88.8 14.3 %collective-permute-start.8 = (f32[16,4992]{1,0:T(8,128)S(1)}, f32[16,4992]{1,0:T(8,128)S(1)}, u32[]{:S(2)}, u32[]{:S(2)}) collective-permute-start(f32[16,4992]{1,0:T(8,128)S(1)} %get-tuple-element.81), channel_id=1, source_target_pairs={{0,128},{1,33},{2,130},{3,35},{4,132},{5,37},{6,134},{7,39},{8,136... | collective-permute-start | bytes 958472 | tf_op jit(solution)/shard_map/ppermute | solution.py:58
  93.8 12.0 %collective-permute-start.23 = (f32[16,4992]{1,0:T(8,128)S(1)}, f32[16,4992]{1,0:T(8,128)S(1)}, u32[]{:S(2)}, u32[]{:S(2)}) collective-permute-start(f32[16,4992]{1,0:T(8,128)S(1)} %get-tuple-element.104), channel_id=1, source_target_pairs={{0,192},{1,49},{2,194},{3,51},{4,196},{5,53},{6,198},{7,55},{8,200... | collective-permute-start | bytes 958472 | tf_op jit(solution)/shard_map/ppermute | solution.py:58
  95.4 11.1 %collective-permute-start.24 = (f32[16,4992]{1,0:T(8,128)S(1)}, f32[16,4992]{1,0:T(8,128)S(1)}, u32[]{:S(2)}, u32[]{:S(2)}) collective-permute-start(f32[16,4992]{1,0:T(8,128)S(1)} %get-tuple-element.105), channel_id=1, source_target_pairs={{0,64},{1,17},{2,66},{3,19},{4,68},{5,21},{6,70},{7,23},{8,72},{9,... | collective-permute-start | bytes 958472 | tf_op jit(solution)/shard_map/ppermute | solution.py:58
  98.1 11.8 %collective-permute-start.25 = (f32[16,4992]{1,0:T(8,128)S(1)}, f32[16,4992]{1,0:T(8,128)S(1)}, u32[]{:S(2)}, u32[]{:S(2)}) collective-permute-start(f32[16,4992]{1,0:T(8,128)S(1)} %get-tuple-element.106), channel_id=1, source_target_pairs={{0,128},{1,33},{2,130},{3,35},{4,132},{5,37},{6,134},{7,39},{8,136... | collective-permute-start | bytes 958472 | tf_op jit(solution)/shard_map/ppermute | solution.py:58
  103.2 9.7 %collective-permute-start.11 = (bf16[16,4992]{1,0:T(8,128)(2,1)S(1)}, bf16[16,4992]{1,0:T(8,128)(2,1)S(1)}, u32[]{:S(2)}, u32[]{:S(2)}) collective-permute-start(bf16[16,4992]{1,0:T(8,128)(2,1)S(1)} %shard_map.133.refs_0_), channel_id=1, source_target_pairs={{0,128},{1,33},{2,130},{3,35},{4,132},{5,37},{6,134},{7,39},{8,136... | collective-permute-start | bytes 479240 | tf_op jit(solution)/shard_map/ppermute | solution.py:58
  104.1 9.8 %collective-permute-start.10 = (bf16[16,4992]{1,0:T(8,128)(2,1)S(1)}, bf16[16,4992]{1,0:T(8,128)(2,1)S(1)}, u32[]{:S(2)}, u32[]{:S(2)}) collective-permute-start(bf16[16,4992]{1,0:T(8,128)(2,1)S(1)} %shard_map.133.refs_0_), channel_id=1, source_target_pairs={{0,64},{1,17},{2,66},{3,19},{4,68},{5,21},{6,70},{7,23},{8,72},{9,... | collective-permute-start | bytes 479240 | tf_op jit(solution)/shard_map/ppermute | solution.py:58
  105.8 8.1 %collective-permute-start.9 = (bf16[16,4992]{1,0:T(8,128)(2,1)S(1)}, bf16[16,4992]{1,0:T(8,128)(2,1)S(1)}, u32[]{:S(2)}, u32[]{:S(2)}) collective-permute-start(bf16[16,4992]{1,0:T(8,128)(2,1)S(1)} %shard_map.133.refs_0_), channel_id=1, source_target_pairs={{0,192},{1,49},{2,194},{3,51},{4,196},{5,53},{6,198},{7,55},{8,200... | collective-permute-start | bytes 479240 | tf_op jit(solution)/shard_map/ppermute | solution.py:58
  110.0 6.0 %collective-permute-start.28 = (bf16[16,4992]{1,0:T(8,128)(2,1)S(1)}, bf16[16,4992]{1,0:T(8,128)(2,1)S(1)}, u32[]{:S(2)}, u32[]{:S(2)}) collective-permute-start(bf16[16,4992]{1,0:T(8,128)(2,1)S(1)} %shard_map.139.refs_0_), channel_id=1, source_target_pairs={{0,128},{1,33},{2,130},{3,35},{4,132},{5,37},{6,134},{7,39},{8,136... | collective-permute-start | bytes 479240 | tf_op jit(solution)/shard_map/ppermute | solution.py:58
  110.9 6.6 %collective-permute-start.27 = (bf16[16,4992]{1,0:T(8,128)(2,1)S(1)}, bf16[16,4992]{1,0:T(8,128)(2,1)S(1)}, u32[]{:S(2)}, u32[]{:S(2)}) collective-permute-start(bf16[16,4992]{1,0:T(8,128)(2,1)S(1)} %shard_map.139.refs_0_), channel_id=1, source_target_pairs={{0,64},{1,17},{2,66},{3,19},{4,68},{5,21},{6,70},{7,23},{8,72},{9,... | collective-permute-start | bytes 479240 | tf_op jit(solution)/shard_map/ppermute | solution.py:58
  112.9 5.6 %collective-permute-start.26 = (bf16[16,4992]{1,0:T(8,128)(2,1)S(1)}, bf16[16,4992]{1,0:T(8,128)(2,1)S(1)}, u32[]{:S(2)}, u32[]{:S(2)}) collective-permute-start(bf16[16,4992]{1,0:T(8,128)(2,1)S(1)} %shard_map.139.refs_0_), channel_id=1, source_target_pairs={{0,192},{1,49},{2,194},{3,51},{4,196},{5,53},{6,198},{7,55},{8,200... | collective-permute-start | bytes 479240 | tf_op jit(solution)/shard_map/ppermute | solution.py:58
  113.9 11.4 %collective-permute-start.12 = (bf16[64,2560]{1,0:T(8,128)(2,1)S(1)}, bf16[64,2560]{1,0:T(8,128)(2,1)S(1)}, u32[]{:S(2)}, u32[]{:S(2)}) collective-permute-start(bf16[64,2560]{1,0:T(8,128)(2,1)S(1)} %get-tuple-element.82.a), channel_id=1, source_target_pairs={{0,48},{1,193},{2,50},{3,195},{4,52},{5,197},{6,54},{7,199},{8,56}... | collective-permute-start | bytes 983048 | tf_op jit(solution)/shard_map/ppermute | solution.py:58
  116.0 9.0 %collective-permute-start.13 = (bf16[64,2432]{1,0:T(8,128)(2,1)S(1)}, bf16[64,2432]{1,0:T(8,128)(2,1)S(1)}, u32[]{:S(2)}, u32[]{:S(2)}) collective-permute-start(bf16[64,2432]{1,0:T(8,128)(2,1)S(1)} %get-tuple-element.83.b), channel_id=1, source_target_pairs={{0,16},{1,65},{2,18},{3,67},{4,20},{5,69},{6,22},{7,71},{8,24},{9,... | collective-permute-start | bytes 933896 | tf_op jit(solution)/shard_map/ppermute | solution.py:58
  118.6 10.8 %collective-permute-start.29 = (bf16[64,2560]{1,0:T(8,128)(2,1)S(1)}, bf16[64,2560]{1,0:T(8,128)(2,1)S(1)}, u32[]{:S(2)}, u32[]{:S(2)}) collective-permute-start(bf16[64,2560]{1,0:T(8,128)(2,1)S(1)} %get-tuple-element.107.a), channel_id=1, source_target_pairs={{0,48},{1,193},{2,50},{3,195},{4,52},{5,197},{6,54},{7,199},{8,56}... | collective-permute-start | bytes 983048 | tf_op jit(solution)/shard_map/ppermute | solution.py:58
  119.9 8.9 %collective-permute-start.30 = (bf16[64,2432]{1,0:T(8,128)(2,1)S(1)}, bf16[64,2432]{1,0:T(8,128)(2,1)S(1)}, u32[]{:S(2)}, u32[]{:S(2)}) collective-permute-start(bf16[64,2432]{1,0:T(8,128)(2,1)S(1)} %get-tuple-element.108.b), channel_id=1, source_target_pairs={{0,16},{1,65},{2,18},{3,67},{4,20},{5,69},{6,22},{7,71},{8,24},{9,... | collective-permute-start | bytes 933896 | tf_op jit(solution)/shard_map/ppermute | solution.py:58
  126.5 12.3 %collective-permute-start.14 = (bf16[128,2560]{1,0:T(8,128)(2,1)}, bf16[128,2560]{1,0:T(8,128)(2,1)}, u32[]{:S(2)}, u32[]{:S(2)}) collective-permute-start(bf16[128,2560]{1,0:T(8,128)(2,1)} %get-tuple-element.84.a.first.refs_0_), channel_id=1, source_target_pairs={{0,16},{1,65},{2,18},{3,67},{4,20},{5,69},{6,22},{7,71},{8,24},{9,... | collective-permute-start | bytes 1966088 | tf_op jit(solution)/shard_map/ppermute | solution.py:58
  127.9 10.9 %collective-permute-start.15 = (bf16[128,2432]{1,0:T(8,128)(2,1)}, bf16[128,2432]{1,0:T(8,128)(2,1)}, u32[]{:S(2)}, u32[]{:S(2)}) collective-permute-start(bf16[128,2432]{1,0:T(8,128)(2,1)} %get-tuple-element.85.b.first.refs_4_), channel_id=1, source_target_pairs={{0,48},{1,193},{2,50},{3,195},{4,52},{5,197},{6,54},{7,199},{8,56}... | collective-permute-start | bytes 1867784 | tf_op jit(solution)/shard_map/ppermute | solution.py:58
  130.6 18.2 %collective-permute-start.31 = (bf16[128,2560]{1,0:T(8,128)(2,1)}, bf16[128,2560]{1,0:T(8,128)(2,1)}, u32[]{:S(2)}, u32[]{:S(2)}) collective-permute-start(bf16[128,2560]{1,0:T(8,128)(2,1)} %get-tuple-element.109.a.third.refs_2_), channel_id=1, source_target_pairs={{0,16},{1,65},{2,18},{3,67},{4,20},{5,69},{6,22},{7,71},{8,24},{9,... | collective-permute-start | bytes 1966088 | tf_op jit(solution)/shard_map/ppermute | solution.py:58
  131.7 17.0 %collective-permute-start.32 = (bf16[128,2432]{1,0:T(8,128)(2,1)}, bf16[128,2432]{1,0:T(8,128)(2,1)}, u32[]{:S(2)}, u32[]{:S(2)}) collective-permute-start(bf16[128,2432]{1,0:T(8,128)(2,1)} %get-tuple-element.110.b.third.refs_6_), channel_id=1, source_target_pairs={{0,48},{1,193},{2,50},{3,195},{4,52},{5,197},{6,54},{7,199},{8,56}... | collective-permute-start | bytes 1867784 | tf_op jit(solution)/shard_map/ppermute | solution.py:58
  144.9 9.1 %copy-start.13 = (bf16[512,512]{1,0:T(8,128)(2,1)S(1)}, bf16[512,512]{1,0:T(8,128)(2,1)}, u32[]{:S(2)}) copy-start(bf16[512,512]{1,0:T(8,128)(2,1)} %copy-done.12) | copy-start | bytes 1572868
  144.9 13.1 %collective-permute-start.16 = (f32[128,1024]{1,0:T(8,128)S(1)}, f32[128,1024]{1,0:T(8,128)S(1)}, u32[]{:S(2)}, u32[]{:S(2)}) collective-permute-start(f32[128,1024]{1,0:T(8,128)S(1)} %get-tuple-element.90), channel_id=1, source_target_pairs={{0,1},{1,0},{2,3},{3,2},{4,5},{5,4},{6,7},{7,6},{8,9},{9,8},{10,11... | collective-permute-start | bytes 1572872 | tf_op jit(solution)/shard_map/ppermute | solution.py:364
  153.3 4.6 %collective-permute-start.33 = (f32[128,1024]{1,0:T(8,128)S(1)}, f32[128,1024]{1,0:T(8,128)S(1)}, u32[]{:S(2)}, u32[]{:S(2)}) collective-permute-start(f32[128,1024]{1,0:T(8,128)S(1)} %get-tuple-element.112), channel_id=1, source_target_pairs={{0,1},{1,0},{2,3},{3,2},{4,5},{5,4},{6,7},{7,6},{8,9},{9,8},{10,11... | collective-permute-start | bytes 1572872 | tf_op jit(solution)/shard_map/ppermute | solution.py:364
  158.1 12.9 %collective-permute-start.34 = (bf16[32,1024]{1,0:T(8,128)(2,1)S(1)}, bf16[32,1024]{1,0:T(8,128)(2,1)S(1)}, u32[]{:S(2)}, u32[]{:S(2)}) collective-permute-start(bf16[32,1024]{1,0:T(8,128)(2,1)S(1)} %get-tuple-element.114), channel_id=1, source_target_pairs={{0,2},{1,3},{2,4},{3,5},{4,6},{5,7},{6,8},{7,9},{8,10},{9,11},{10,... | collective-permute-start | bytes 196616 | tf_op jit(solution)/shard_map/ppermute | solution.py:367
  159.2 14.2 %collective-permute-start.35 = (bf16[32,1024]{1,0:T(8,128)(2,1)S(1)}, bf16[32,1024]{1,0:T(8,128)(2,1)S(1)}, u32[]{:S(2)}, u32[]{:S(2)}) collective-permute-start(bf16[32,1024]{1,0:T(8,128)(2,1)S(1)} %get-tuple-element.115), channel_id=1, source_target_pairs={{0,4},{1,5},{2,6},{3,7},{4,8},{5,9},{6,10},{7,11},{8,12},{9,13},{1... | collective-permute-start | bytes 196616 | tf_op jit(solution)/shard_map/ppermute | solution.py:367
  159.2 15.0 %copy-start.15 = (bf16[512,512]{1,0:T(8,128)(2,1)S(1)}, bf16[512,512]{1,0:T(8,128)(2,1)}, u32[]{:S(2)}) copy-start(bf16[512,512]{1,0:T(8,128)(2,1)} %copy-done.14) | copy-start | bytes 1572868
  159.2 15.0 %copy-start.17 = (bf16[512,512]{1,0:T(8,128)(2,1)S(1)}, bf16[512,512]{1,0:T(8,128)(2,1)}, u32[]{:S(2)}) copy-start(bf16[512,512]{1,0:T(8,128)(2,1)} %copy-done.16) | copy-start | bytes 1572868
  163.3 15.5 %collective-permute-start.36 = (bf16[32,1024]{1,0:T(8,128)(2,1)S(1)}, bf16[32,1024]{1,0:T(8,128)(2,1)S(1)}, u32[]{:S(2)}, u32[]{:S(2)}) collective-permute-start(bf16[32,1024]{1,0:T(8,128)(2,1)S(1)} %get-tuple-element.116), channel_id=1, source_target_pairs={{0,6},{1,7},{2,8},{3,9},{4,10},{5,11},{6,12},{7,13},{8,14},{9,15},... | collective-permute-start | bytes 196616 | tf_op jit(solution)/shard_map/ppermute | solution.py:367
  165.4 13.4 %collective-permute-start.37 = (bf16[32,1024]{1,0:T(8,128)(2,1)S(1)}, bf16[32,1024]{1,0:T(8,128)(2,1)S(1)}, u32[]{:S(2)}, u32[]{:S(2)}) collective-permute-start(bf16[32,1024]{1,0:T(8,128)(2,1)S(1)} %get-tuple-element.117), channel_id=1, source_target_pairs={{0,8},{1,9},{2,10},{3,11},{4,12},{5,13},{6,14},{7,15},{8,0},{9,1},... | collective-permute-start | bytes 196616 | tf_op jit(solution)/shard_map/ppermute | solution.py:367
  168.8 10.1 %collective-permute-start.38 = (bf16[32,1024]{1,0:T(8,128)(2,1)S(1)}, bf16[32,1024]{1,0:T(8,128)(2,1)S(1)}, u32[]{:S(2)}, u32[]{:S(2)}) collective-permute-start(bf16[32,1024]{1,0:T(8,128)(2,1)S(1)} %get-tuple-element.118), channel_id=1, source_target_pairs={{0,10},{1,11},{2,12},{3,13},{4,14},{5,15},{6,0},{7,1},{8,2},{9,3},... | collective-permute-start | bytes 196616 | tf_op jit(solution)/shard_map/ppermute | solution.py:367
  171.0 11.0 %collective-permute-start.39 = (bf16[32,1024]{1,0:T(8,128)(2,1)S(1)}, bf16[32,1024]{1,0:T(8,128)(2,1)S(1)}, u32[]{:S(2)}, u32[]{:S(2)}) collective-permute-start(bf16[32,1024]{1,0:T(8,128)(2,1)S(1)} %get-tuple-element.119), channel_id=1, source_target_pairs={{0,12},{1,13},{2,14},{3,15},{4,0},{5,1},{6,2},{7,3},{8,4},{9,5},{1... | collective-permute-start | bytes 196616 | tf_op jit(solution)/shard_map/ppermute | solution.py:367
  173.4 8.6 %collective-permute-start.40 = (bf16[32,1024]{1,0:T(8,128)(2,1)S(1)}, bf16[32,1024]{1,0:T(8,128)(2,1)S(1)}, u32[]{:S(2)}, u32[]{:S(2)}) collective-permute-start(bf16[32,1024]{1,0:T(8,128)(2,1)S(1)} %get-tuple-element.120), channel_id=1, source_target_pairs={{0,14},{1,15},{2,0},{3,1},{4,2},{5,3},{6,4},{7,5},{8,6},{9,7},{10,... | collective-permute-start | bytes 196616 | tf_op jit(solution)/shard_map/ppermute | solution.py:367
  (22 other events, 64.4 us)

commit v2 on v1

v2 whole, which is shorter than its diff:
```python
import math

import jax
import jax.numpy as jnp
from jax import lax
from jax.experimental import pallas as pl
from jax.experimental.pallas import tpu as pltpu
from jax.sharding import PartitionSpec as P

F32 = jnp.float32
BF16 = jnp.bfloat16
BOTH = ("row", "col")


GRAY_A = (0, 1, 1, 0)
GRAY_B = (0, 0, 1, 1)
WIDE = 1664
SPLIT = 896
PART_A = WIDE + SPLIT
PART_B = WIDE + WIDE - SPLIT
ROOM = 6 * 1024 * 1024


def code_of(y, x, core):
    along_x = 2 * GRAY_A[x] + GRAY_B[x]
    along_y = 2 * GRAY_A[y] + GRAY_B[y]
    return 4 * along_x + along_y if core == 0 else 4 * along_y + along_x


PLACE = {
    (code_of(y, x, core), core): y * 4 + x
    for y in range(4)
    for x in range(4)
    for core in range(2)
}


def flips(mask):
    pairs = []
    for row in range(16):
        for col in range(16):
            code = code_of(row // 4, row % 4, col % 2)
            pairs.append((row * 16 + col, PLACE[(code ^ mask, col % 2)] * 16 + col))
    return pairs


FLIPS = {mask: flips(mask) for mask in (1, 2, 3, 4, 8)}
CORES = [(i, i ^ 1) for i in range(16)]


def turn_by(shift):
    return [(i, (i + 2 * shift) % 16) for i in range(16)]


def fan_by(shift):
    return [(i, (i + (2 - 4 * (i % 2)) * shift) % 16) for i in range(16)]


def send(x, mask):
    return lax.ppermute(x, BOTH, FLIPS[mask])


def tiles(start, stop):
    return [(at, min(at + 256, stop)) for at in range(start, stop, 256)]


def nn(left, right):
    return lax.dot_general(left, right, (((1,), (0,)), ((), ())), preferred_element_type=F32)


def tn(left, right):
    return lax.dot_general(left, right, (((0,), (0,)), ((), ())), preferred_element_type=F32)


def run(kernel, outs, arrays, smem=0, far=(), scratch=(), flops=0):
    shapes = [jax.ShapeDtypeStruct(shape, kind) for shape, kind in outs]
    moved = sum(math.prod(a.shape) * a.dtype.itemsize for a in (*arrays, *shapes))
    held = moved + sum(
        math.prod(s.shape) * jnp.dtype(s.dtype).itemsize for s in scratch if len(s.shape) > 1
    )
    places = [pltpu.SMEM if k < smem else pltpu.VMEM for k in range(len(arrays) + len(outs))]
    for k in far:
        places[k] = pl.ANY
    specs = [pl.BlockSpec(memory_space=place) for place in places]
    return pl.pallas_call(
        kernel,
        out_shape=shapes,
        in_specs=specs[: len(arrays)],
        out_specs=specs[len(arrays) :],
        scratch_shapes=list(scratch),
        compiler_params=pltpu.CompilerParams(vmem_limit_bytes=held + ROOM),
        cost_estimate=pl.CostEstimate(flops=flops, bytes_accessed=moved, transcendentals=0),
    )(*arrays)


def stack_kernel(*refs):
    at = 0
    for ref in refs[:-1]:
        refs[-1][pl.ds(at, ref.shape[0]), :] = ref[...]
        at += ref.shape[0]


def stack(*arrays):
    height = sum(a.shape[0] for a in arrays)
    return run(stack_kernel, [((height, arrays[0].shape[1]), arrays[0].dtype)], arrays)[0]


def pair_kernel(both, other, out):
    for which in range(2):
        rows = pl.ds(32 * which, 32)
        out[pl.ds(64 * which, 32), :] = both[rows, :]
        out[pl.ds(64 * which + 32, 32), :] = other[rows, :]


def pair_up(*arrays):
    return run(pair_kernel, [((128, 512), BF16)], arrays)[0]


def arrange_kernel(index_a, index_b, pair, near_1, near_2, near_3, four, post, *refs):
    outs, panel = refs[:-1], refs[-1]
    for which in range(2):
        here = 64 * which
        for slot, ref in enumerate((pair, near_1, near_2, near_3)):
            panel[pl.ds(64 * slot, 64), :] = ref[pl.ds(here, 64), :]
        panel[pl.ds(256, 32), :] = four[pl.ds(32 * which, 32), :]
        panel[pl.ds(288, 32), :] = post[pl.ds(384 + 32 * which, 32), :]
        for k in (1, 2, 3):
            at, start = 64 * (8 - k), 128 * (k - 1) + here
            panel[pl.ds(at + 32, 32), :] = post[pl.ds(start, 32), :]
            panel[pl.ds(at, 32), :] = post[pl.ds(start + 32, 32), :]
        for index, out in zip((index_a, index_b), outs[2 * which : 2 * which + 2]):
            for part in range(2):
                for j in range(16):
                    start = pl.multiple_of(index[j] * 32 + part * 16, 16)
                    out[pl.ds(part * 256 + j * 16, 16), :] = panel[pl.ds(start, 16), :]


def arrange(*arrays):
    return run(
        arrange_kernel,
        [((512, 512), BF16)] * 4,
        arrays,
        smem=2,
        scratch=[pltpu.VMEM((512, 512), BF16)],
    )


def scale_kernel(scale, quant, weight, turned):
    block_rows, block_columns = scale.shape
    for r in range(block_rows):
        for c in range(block_columns):
            rows, columns = pl.ds(r * 128, 128), pl.ds(c * 128, 128)
            block = (quant[rows, columns].astype(F32) * scale[r, c]).astype(BF16)
            weight[rows, columns] = block
            turned[columns, rows] = jnp.transpose(block)


def scaled(scale, quant):
    outs = [(quant.shape, BF16), (quant.shape[::-1], BF16)]
    return run(scale_kernel, outs, [scale, quant], smem=1)


def first_kernel(tokens_a, tokens_b, grads_a, grads_b, gate, up, down, *outs):
    a, b = outs[:4], outs[4:]
    for panel, weight, first, last, shift, (keep_0, give_0, keep_1, give_1) in (
        (tokens_a, gate, 0, WIDE, 0, a),
        (tokens_b, up, 0, WIDE, 0, b),
        (grads_a, down, 0, SPLIT, WIDE, a),
        (grads_b, down, SPLIT, WIDE, WIDE - SPLIT, b),
    ):
        for at, stop in tiles(first, last):
            product = nn(panel[...], weight[:, at:stop])
            columns = pl.ds(at + shift, stop - at)
            keep_0[:, columns] = product[:128]
            give_0[:, columns] = product[128:256].astype(BF16)
            keep_1[:, columns] = product[256:384]
            give_1[:, columns] = product[384:].astype(BF16)


def first(*arrays):
    outs = []
    for width in (PART_A, PART_B):
        outs += [((128, width), F32), ((128, width), BF16)] * 2
    return run(first_kernel, outs, arrays, flops=3 * 2 * 512 * 512 * WIDE)


def second_kernel(held_a, came_a, held_b, came_b, keep_a, give_a, keep_b, give_b):
    for held, came, keep, give in (
        (held_a, came_a, keep_a, give_a),
        (held_b, came_b, keep_b, give_b),
    ):
        keep[...] = held[:64] + came[:64].astype(F32)
        give[...] = (held[64:] + came[64:].astype(F32)).astype(give.dtype)


def second(*arrays):
    outs = [((64, width), kind) for width in (PART_A, PART_B) for kind in (F32, BF16)]
    return run(second_kernel, outs, arrays)


def third_kernel(held_a, came_a, held_b, came_b, *outs):
    for j in range(4):
        rows = pl.ds(16 * j, 16)
        outs[j][:, :PART_A] = held_a[rows, :] + came_a[rows, :].astype(F32)
        outs[j][:, PART_A:] = held_b[rows, :] + came_b[rows, :].astype(F32)


def third(*arrays):
    return run(third_kernel, [((16, PART_A + PART_B), F32)] * 4, arrays)


def middle_kernel(held, came_1, came_2, came_3, out):
    def total(at, stop):
        return (held[:, at:stop] + came_1[:, at:stop]) + (came_2[:, at:stop] + came_3[:, at:stop])

    for at, stop in [(0, SPLIT), (SPLIT, WIDE)]:
        gate = total(at, stop)
        up = total(PART_A + at, PART_A + stop)
        offset = WIDE if at == 0 else PART_A + WIDE - SPLIT
        back = total(offset + at, offset + stop)
        sigmoid = 1.0 / (1.0 + jnp.exp(-gate))
        activated = gate * sigmoid
        out[:, offset + at : offset + stop] = (activated * up).astype(BF16)
        slope = sigmoid * (1.0 + gate * (1.0 - sigmoid))
        out[:, at:stop] = (back * up * slope).astype(BF16)
        out[:, PART_A + at : PART_A + stop] = (back * activated).astype(BF16)


def middle(*arrays):
    return run(middle_kernel, [((16, PART_A + PART_B), BF16)], arrays)[0]


def spread_kernel(*refs):
    ins, (out_a, out_b) = refs[:4], refs[4:]
    for j in range(4):
        out_a[pl.ds(16 * j, 16), :] = ins[j][:, :PART_A]
        out_b[pl.ds(16 * j, 16), :] = ins[j][:, PART_A:]


def spread(*arrays):
    return run(spread_kernel, [((64, PART_A), BF16), ((64, PART_B), BF16)], arrays)


def join_kernel(a, came_a, b, came_b, out_a, out_b):
    out_a[:64, :] = a[...]
    out_a[64:, :] = came_a[...]
    out_b[:64, :] = b[...]
    out_b[64:, :] = came_b[...]


def join(*arrays):
    return run(join_kernel, [((128, PART_A), BF16), ((128, PART_B), BF16)], arrays)


def project_kernel(index_a, index_b, a, came_a, b, came_b, gate, up, down, keep, give, sum_a, sum_b):
    left = jnp.concatenate([a[...], came_a[...]], axis=0)
    right = jnp.concatenate([b[...], came_b[...]], axis=0)
    sum_a[:, :512] = nn(left[:, WIDE:], down[:SPLIT, :])
    sum_b[:, :512] = nn(right[:, WIDE:], down[SPLIT:, :])
    sum_a[:, 512:] = nn(left[:, :WIDE], gate[...])
    sum_b[:, 512:] = nn(right[:, :WIDE], up[...])
    for k in range(16):
        out = keep if k < 8 else give
        from_a = pl.multiple_of(index_a[k] * 16, 16)
        from_b = pl.multiple_of(index_b[k] * 16, 16)
        out[pl.ds((k % 8) * 16, 16), :] = (
            sum_a[pl.ds(from_a, 16), :] + sum_b[pl.ds(from_b, 16), :]
        )


def project(*arrays):
    return run(
        project_kernel,
        [((128, 1024), F32)] * 2,
        arrays,
        smem=2,
        scratch=[pltpu.VMEM((256, 1024), F32)] * 2,
        flops=3 * 2 * 256 * 512 * WIDE,
    )


def chunk_kernel(keep_0, came_0, keep_1, came_1, own, *outs):
    for k in range(8):
        rows = pl.ds(16 * k, 16)
        out, at = (outs[k // 2], 32 * (k % 2)) if k < 6 else (outs[3] if k == 6 else own, 0)
        out[pl.ds(at, 16), :] = (keep_0[rows, :] + came_0[rows, :]).astype(out.dtype)
        out[pl.ds(at + 16, 16), :] = (keep_1[rows, :] + came_1[rows, :]).astype(out.dtype)


def chunk(*arrays):
    outs = [((32, 1024), F32)] + [((64, 1024), BF16)] * 3 + [((32, 1024), BF16)]
    return run(chunk_kernel, outs, arrays)


def gather_kernel(own, came_1, came_2, came_3, came_4, mine, other):
    total = [ref[...].astype(F32) for ref in (came_1, came_2, came_3)]
    total = total[0] + total[1] + total[2]
    mine[...] = own[...] + came_4[...].astype(F32) + total[:32]
    other[...] = total[32:]


def gather(*arrays):
    return run(gather_kernel, [((32, 1024), F32)] * 2, arrays)


def finish_kernel(mine, came, output, input_grad):
    output[...] = (mine[:, :512] + came[:, :512]).astype(BF16)
    input_grad[...] = (mine[:, 512:] + came[:, 512:]).astype(BF16)


def finish(*arrays):
    return run(finish_kernel, [((32, 512), BF16)] * 2, arrays)


def weight_grads_kernel(tokens_a, tokens_b, grads_a, grads_b, *refs):
    parts_a, parts_b, (gate, up, down) = refs[:4], refs[4:8], refs[8:11]
    held_a, held_b, wide, tall, came, gone = refs[11:]
    loads = []
    for parts, held in ((parts_a, held_a), (parts_b, held_b)):
        for k in range(4):
            load = pltpu.make_async_copy(
                parts[k], held.at[pl.ds(128 * k, 128), :], came.at[len(loads)]
            )
            load.start()
            loads.append(load)
    stores = []

    def store(source, target):
        copy = pltpu.make_async_copy(source, target, gone.at[len(stores)])
        copy.start()
        stores.append(copy)

    for which, (tokens, grads, held, out, first, last) in enumerate(
        (
            (tokens_a, grads_a, held_a, gate, 0, SPLIT),
            (tokens_b, grads_b, held_b, up, SPLIT, WIDE),
        )
    ):
        turned = jnp.transpose(tokens[...])
        for load in loads[4 * which : 4 * which + 4]:
            load.wait()
        for at, stop in ((0, 512), (512, 1024), (1024, WIDE)):
            columns = pl.ds(at, stop - at)
            wide[which, :, columns] = nn(turned, held[:, columns]).astype(BF16)
            store(wide.at[which, :, columns], out.at[:, columns])
        rows = pl.ds(first, last - first)
        tall[rows, :] = tn(held[:, WIDE:], grads[...]).astype(BF16)
        store(tall.at[rows, :], down.at[rows, :])
    for copy in stores:
        copy.wait()


def weight_grads(*arrays):
    return run(
        weight_grads_kernel,
        [((512, WIDE), BF16), ((512, WIDE), BF16), ((WIDE, 512), BF16)],
        arrays,
        far=range(4, 15),
        scratch=[
            pltpu.VMEM((512, PART_A), BF16),
            pltpu.VMEM((512, PART_B), BF16),
            pltpu.VMEM((2, 512, WIDE), BF16),
            pltpu.VMEM((WIDE, 512), BF16),
            pltpu.SemaphoreType.DMA((8,)),
            pltpu.SemaphoreType.DMA((8,)),
        ],
        flops=3 * 2 * 512 * 512 * WIDE,
    )


def local(tokens, gate_quant, gate_scale, up_quant, up_scale, down_quant, down_scale, out_grad):
    both = stack(tokens, out_grad)
    pair = pair_up(both, lax.ppermute(both, "col", CORES))
    near = [lax.ppermute(pair, "col", fan_by(k)) for k in (3, 2, 1)][::-1]
    four = lax.ppermute(both, "col", turn_by(4))
    pair, row, col, up_quant, gate_quant, down_quant, down_scale = lax.optimization_barrier(
        (pair, lax.axis_index("row"), lax.axis_index("col"))
        + (up_quant, gate_quant, down_quant, down_scale)
    )
    core = lax.rem(col, 2)
    depth = lax.div(col, 2)
    table = jnp.array(
        [[code_of(r // 4, r % 4, c) for c in range(2)] for r in range(16)], jnp.int32
    )
    code = table[row, core]
    blocks = jnp.arange(16, dtype=jnp.int32)

    def swapped(j):
        return (j & 3) | (((j >> 2) & 1) << 3) | (((j >> 3) & 1) << 2)

    def place(group):
        away = (group >> 1) - depth
        slot = jnp.where(core == 0, -away, away) & 7
        return 2 * slot + ((group & 1) ^ core)

    index_a = place(blocks ^ code)
    index_b = place(swapped(blocks) ^ code)
    shift = jnp.array([1, 1, 2, 2, 3, 3, 4, 0] * 2, jnp.int32)
    flip = jnp.array([0, 1, 0, 1, 0, 1, 0, 0] * 2, jnp.int32)
    owner = core ^ (blocks >> 3)
    target = (depth + jnp.where(owner == 0, shift, -shift)) & 7
    home_a = (2 * target + (owner ^ flip)) ^ code
    home_b = swapped(home_a)

    w_up, w_up_turned = scaled(up_scale, up_quant)
    w_gate, w_gate_turned = scaled(gate_scale, gate_quant)
    w_down, w_down_turned = scaled(down_scale, down_quant)
    four, index_a, index_b, home_a, home_b, w_up, w_gate, w_down_turned = lax.optimization_barrier(
        (four, index_a, index_b, home_a, home_b, w_up, w_gate, w_down_turned)
    )
    post = lax.ppermute(stack(*near, four), "col", CORES)
    tokens_a, tokens_b, grads_a, grads_b = arrange(index_a, index_b, pair, *near, four, post)
    parts = first(tokens_a, tokens_b, grads_a, grads_b, w_gate, w_up, w_down_turned)
    state = []
    for part in range(2):
        keep_a, give_a, keep_b, give_b = *parts[2 * part : 2 * part + 2], *parts[4 + 2 * part : 6 + 2 * part]
        state.append((keep_a, send(give_a, 8), keep_b, send(give_b, 4)))
    for part in range(2):
        keep_a, give_a, keep_b, give_b = second(*state[part])
        state[part] = (keep_a, send(give_a, 4), keep_b, send(give_b, 8))
    for part in range(2):
        held, *give = third(*state[part])
        state[part] = (held, *(send(give[j - 1], j) for j in (1, 2, 3)))
    for part in range(2):
        own = middle(*state[part])
        state[part] = (own, *(send(own, j) for j in (1, 2, 3)))
    for part in range(2):
        a, b = spread(*state[part])
        state[part] = (a, send(a, 4), b, send(b, 8))
    for part in range(2):
        a, b = join(*state[part])
        state[part] = (a, send(a, 8), b, send(b, 4))
    ends = []
    for part in range(2):
        keep, give = project(home_a, home_b, *state[part], w_gate_turned, w_up_turned, w_down)
        ends += [keep, lax.ppermute(give, "col", CORES)]
    own, *sent = chunk(*ends)
    own, tokens_a, tokens_b, grads_a, grads_b = lax.optimization_barrier(
        (own, tokens_a, tokens_b, grads_a, grads_b)
    )
    last = [lax.ppermute(sent[k - 1], "col", fan_by(k)) for k in (3, 2, 1)][::-1]
    last.append(lax.ppermute(sent[3], "col", turn_by(4)))
    all_a = [*state[0][:2], *state[1][:2]]
    all_b = [*state[0][2:], *state[1][2:]]
    gate_grad, up_grad, down_grad = weight_grads(
        tokens_a, tokens_b, grads_a, grads_b, *all_a, *all_b
    )
    own, gate_grad, up_grad, down_grad = lax.optimization_barrier(
        (own, gate_grad, up_grad, down_grad)
    )
    mine, other = gather(own, *last)
    output, input_grad = finish(mine, lax.ppermute(other, "col", CORES))
    return (output, input_grad, gate_grad, up_grad, down_grad)


def solution(mesh):
    placed = (
        P("col", "row"),
        P("row", "col"),
        P("row", "col"),
        P("row", "col"),
        P("row", "col"),
        P("col", "row"),
        P("col", "row"),
        P("col", "row"),
    )
    return jax.shard_map(
        local,
        mesh=mesh,
        in_specs=placed,
        out_specs=(
            P("col", "row"),
            P("col", "row"),
            P("row", "col"),
            P("row", "col"),
            P("col", "row"),
        ),
        check_vma=False,
    )
```

time: 183 us -> 135 us (0.74)
  blocking collectives: 39 us -> 0 us
  starting transfers between devices: 48 us -> 69 us
  Pallas kernels: 34.3 us -> 19.9 us
  local copies, waits for them, and re-layouts: 15.1 us -> 5.21 us
  waiting for transfers between devices: 44.1 us -> 38 us
    all_gather x2 -> x0, blocking collectives: 39 us -> none  [the longest x1 23 us: local(): panel = lax.all_gather(tokens, 'col', axis=0, tiled=True)]
    pallas_call x20 -> x24, Pallas kernels: 34.3 us -> 19.9 us  [run(): pl.pallas_call(kernel, out_shape=shapes, in_specs=specs[:len(arrays)], ou...]
    ppermute x7 -> x11, starting transfers between devices: 11.9 us -> 25.4 us  [the longest x1 5.19 us: local(): four = lax.ppermute(both, 'col', turn_by(4))]
    unnamed x59 -> x14, local copies, waits for them, and re-layouts: 13.9 us -> 3.17 us
    ppermute x32 -> x28, waiting for transfers between devices: 41 us -> 33.2 us  [send(): return lax.ppermute(x, BOTH, FLIPS[mask])]
    ppermute x2, starting transfers between devices: 4.52 us -> 9.67 us  [local(): ends += [keep, lax.ppermute(give, 'col', CORES)]]
    ppermute x32 -> x28, starting transfers between devices: 31.5 us -> 33.9 us  [send(): return lax.ppermute(x, BOTH, FLIPS[mask])]
  transfers between devices with their start and end apart: 41 -> 41, of which waited for: 17 -> 17; matrix products, arithmetic and copies ran while one was open for 0% -> 3% of each run, Pallas kernels for 17% -> 11%
where the time goes in v2:
time: 135 us
  starting transfers between devices  69 us (51%)
  waiting for transfers between devices  38 us (28%)
  Pallas kernels  19.9 us (15%)
  local copies, waits for them, and re-layouts  5.21 us (4%)
  other arithmetic  2.01 us (1%)
    ppermute x28, starting transfers between devices, send(): return lax.ppermute(x, BOTH, FLIPS[mask])  33.9 us
    ppermute x28, waiting for transfers between devices, send(): return lax.ppermute(x, BOTH, FLIPS[mask])  33.2 us
    pallas_call x24, Pallas kernels, run(): pl.pallas_call(kernel, out_shape=shapes, in_specs=specs[:len(arrays)], ou...  19.9 us
    ppermute x2, starting transfers between devices, local(): ends += [keep, lax.ppermute(give, 'col', CORES)]  9.67 us
    ppermute x1, starting transfers between devices, local(): four = lax.ppermute(both, 'col', turn_by(4))  5.19 us
    ppermute x1, starting transfers between devices, local(): output, input_grad = finish(mine, lax.ppermute(other, 'col', CORES))  5.06 us
    ppermute x3, starting transfers between devices, local(): near = [lax.ppermute(pair, 'col', fan_by(k)) for k in (3, 2, 1)][::-1]  4.84 us
    ppermute x3, starting transfers between devices, local(): lax.ppermute(sent[k - 1], 'col', fan_by(k))  3.55 us
  transfers between devices with their start and end apart: 41, of which 17 were waited for; matrix products, arithmetic and copies ran while one was open for 3% of the time, Pallas kernels for 11%

profile of v2, /device:TPU:1, one launch (start us, length us, event | category | flops | bytes accessed | tf_op | source)
XLA Modules:
  0.0 135.0 jit_solution(9220869609040593884)
XLA Ops:
  2.2 3.3 %collective-permute-start.1 = (bf16[64,512]{1,0:T(8,128)(2,1)S(1)}, bf16[64,512]{1,0:T(8,128)(2,1)S(1)}, u32[]{:S(2)}, u32[]{:S(2)}) collective-permute-start(bf16[64,512]{1,0:T(8,128)(2,1)S(1)} %shard_map.146.both), channel_id=1, source_target_pairs={{0,1},{1,0},{2,3},{3,2},{4,5},{5,4},{6,7},{7,6},{8,9},{9,8},{10,11... | collective-permute-start | bytes 196616 | tf_op jit(solution)/shard_map/ppermute | solution.py:373
  5.5 5.2 %collective-permute-start = (bf16[64,512]{1,0:T(8,128)(2,1)S(1)}, bf16[64,512]{1,0:T(8,128)(2,1)S(1)}, u32[]{:S(2)}, u32[]{:S(2)}) collective-permute-start(bf16[64,512]{1,0:T(8,128)(2,1)S(1)} %shard_map.146.both), channel_id=1, source_target_pairs={{0,8},{1,9},{2,10},{3,11},{4,12},{5,13},{6,14},{7,15},{8,0},{9,1},... | collective-permute-start | bytes 196616 | tf_op jit(solution)/shard_map/ppermute | solution.py:375
  11.2 3.6 %collective-permute-start.3 = (bf16[128,512]{1,0:T(8,128)(2,1)S(1)}, bf16[128,512]{1,0:T(8,128)(2,1)S(1)}, u32[]{:S(2)}, u32[]{:S(2)}) collective-permute-start(bf16[128,512]{1,0:T(8,128)(2,1)S(1)} %shard_map.147.pair), channel_id=1, source_target_pairs={{0,4},{1,13},{2,6},{3,15},{4,8},{5,1},{6,10},{7,3},{8,12},{9,5},{1... | collective-permute-start | bytes 393224 | tf_op jit(solution)/shard_map/ppermute | solution.py:374
  15.5 1.3 dynamic_slice.3
  16.8 1.4 %shift-left_or_fusion = (s32[16]{0:T(128)S(1)}, s32[16]{0:T(128)S(1)}, s32[16]{0:T(128)S(1)}) fusion(s32[]{:T(128)} %bitcast, s32[16]{0:T(128)} %constant.33.clone, s32[16]{0:T(128)} %constant.32.clone, s32[16]{0:T(128)} %constant.37, s32[]{:T(128)S(6)} %rem.18, s32[]{:T(128)S(6)} %div.9, pred[]{:T(512)S(6)} %eq.7), kind=kLoop, calls=%fused_computation.20 | loop fusion | flops 592 | bytes 397 | tf_op jit(solution)/shard_map/or | solution.py:389
  18.9 1.5 %copy-done = bf16[1664,512]{1,0:T(8,128)(2,1)S(1)} copy-done((bf16[1664,512]{1,0:T(8,128)(2,1)S(1)}, bf16[1664,512]{1,0:T(8,128)(2,1)}, u32[]{:S(2)}) %copy-start) | copy-done | bytes 1703960
  20.4 1.2 shard_map.150
  21.8 1.1 shard_map.148
  23.0 1.1 shard_map.149
  25.4 1.4 %collective-permute-done.5.post = bf16[448,512]{1,0:T(8,128)(2,1)S(1)} collective-permute-done((bf16[448,512]{1,0:T(8,128)(2,1)S(1)}, bf16[448,512]{1,0:T(8,128)(2,1)S(1)}, u32[]{:S(2)}, u32[]{:S(2)}) %collective-permute-start.5) | collective-permute-done | bytes 458784 | tf_op jit(solution)/shard_map/ppermute | solution.py:411
  27.6 3.0 %shard_map.153 = (f32[128,2560]{1,0:T(8,128)S(1)}, bf16[128,2560]{1,0:T(8,128)(2,1)S(1)}, f32[128,2560]{1,0:T(8,128)S(1)}, bf16[128,2560]{1,0:T(8,128)(2,1)S(1)}...) custom-call(bf16[512,512]{1,0:T(8,128)(2,1)S(1)} %get-tuple-element., ...), custom_call_target="tpu_custom_call" | custom-call | flops 2617245696 | bytes 14876672 | tf_op jit(solution)/shard_map/pallas_call | solution.py:85
  30.6 1.4 %collective-permute-start.21 = (bf16[128,2560]{1,0:T(8,128)(2,1)S(1)}, bf16[128,2560]{1,0:T(8,128)(2,1)S(1)}, u32[]{:S(2)}, u32[]{:S(2)}) collective-permute-start(bf16[128,2560]{1,0:T(8,128)(2,1)S(1)} %get-tuple-element.131), channel_id=1, source_target_pairs={{0,16},{1,65},{2,18},{3,67},{4,20},{5,69},{6,22},{7,71},{8,24},{9,... | collective-permute-start | bytes 1966088 | tf_op jit(solution)/shard_map/ppermute | solution.py:60
  32.0 1.9 %collective-permute-start.22 = (bf16[128,2432]{1,0:T(8,128)(2,1)S(1)}, bf16[128,2432]{1,0:T(8,128)(2,1)S(1)}, u32[]{:S(2)}, u32[]{:S(2)}) collective-permute-start(bf16[128,2432]{1,0:T(8,128)(2,1)S(1)} %get-tuple-element.133), channel_id=1, source_target_pairs={{0,48},{1,193},{2,50},{3,195},{4,52},{5,197},{6,54},{7,199},{8,56}... | collective-permute-start | bytes 1867784 | tf_op jit(solution)/shard_map/ppermute | solution.py:60
  34.9 7.7 %collective-permute-done.22.came_b = bf16[128,2432]{1,0:T(8,128)(2,1)S(1)} collective-permute-done((bf16[128,2432]{1,0:T(8,128)(2,1)S(1)}, bf16[128,2432]{1,0:T(8,128)(2,1)S(1)}, u32[]{:S(2)}, u32[]{:S(2)}) %collective-permute-start.22) | collective-permute-done | bytes 622624 | tf_op jit(solution)/shard_map/ppermute | solution.py:60
  42.8 2.0 %collective-permute-start.23 = (bf16[64,2560]{1,0:T(8,128)(2,1)S(1)}, bf16[64,2560]{1,0:T(8,128)(2,1)S(1)}, u32[]{:S(2)}, u32[]{:S(2)}) collective-permute-start(bf16[64,2560]{1,0:T(8,128)(2,1)S(1)} %get-tuple-element.135), channel_id=1, source_target_pairs={{0,48},{1,193},{2,50},{3,195},{4,52},{5,197},{6,54},{7,199},{8,56}... | collective-permute-start | bytes 983048 | tf_op jit(solution)/shard_map/ppermute | solution.py:60
  44.8 4.5 %collective-permute-done.7.came_b = bf16[128,2432]{1,0:T(8,128)(2,1)S(1)} collective-permute-done((bf16[128,2432]{1,0:T(8,128)(2,1)S(1)}, bf16[128,2432]{1,0:T(8,128)(2,1)S(1)}, u32[]{:S(2)}, u32[]{:S(2)}) %collective-permute-start.7) | collective-permute-done | bytes 622624 | tf_op jit(solution)/shard_map/ppermute | solution.py:60
  49.5 2.0 %collective-permute-start.8 = (bf16[64,2560]{1,0:T(8,128)(2,1)S(1)}, bf16[64,2560]{1,0:T(8,128)(2,1)S(1)}, u32[]{:S(2)}, u32[]{:S(2)}) collective-permute-start(bf16[64,2560]{1,0:T(8,128)(2,1)S(1)} %get-tuple-element.114), channel_id=1, source_target_pairs={{0,48},{1,193},{2,50},{3,195},{4,52},{5,197},{6,54},{7,199},{8,56}... | collective-permute-start | bytes 983048 | tf_op jit(solution)/shard_map/ppermute | solution.py:60
  51.5 1.3 collective-permute-done.23.came_a
  52.9 2.6 %collective-permute-start.25 = (f32[16,4992]{1,0:T(8,128)S(1)}, f32[16,4992]{1,0:T(8,128)S(1)}, u32[]{:S(2)}, u32[]{:S(2)}) collective-permute-start(f32[16,4992]{1,0:T(8,128)S(1)} %get-tuple-element.139), channel_id=1, source_target_pairs={{0,192},{1,49},{2,194},{3,51},{4,196},{5,53},{6,198},{7,55},{8,200... | collective-permute-start | bytes 958472 | tf_op jit(solution)/shard_map/ppermute | solution.py:60
  55.5 1.4 %collective-permute-start.27 = (f32[16,4992]{1,0:T(8,128)S(1)}, f32[16,4992]{1,0:T(8,128)S(1)}, u32[]{:S(2)}, u32[]{:S(2)}) collective-permute-start(f32[16,4992]{1,0:T(8,128)S(1)} %get-tuple-element.141), channel_id=1, source_target_pairs={{0,128},{1,33},{2,130},{3,35},{4,132},{5,37},{6,134},{7,39},{8,136... | collective-permute-start | bytes 958472 | tf_op jit(solution)/shard_map/ppermute | solution.py:60
  57.6 2.6 %collective-permute-start.10 = (f32[16,4992]{1,0:T(8,128)S(1)}, f32[16,4992]{1,0:T(8,128)S(1)}, u32[]{:S(2)}, u32[]{:S(2)}) collective-permute-start(f32[16,4992]{1,0:T(8,128)S(1)} %get-tuple-element.118), channel_id=1, source_target_pairs={{0,192},{1,49},{2,194},{3,51},{4,196},{5,53},{6,198},{7,55},{8,200... | collective-permute-start | bytes 958472 | tf_op jit(solution)/shard_map/ppermute | solution.py:60
  60.2 2.0 %collective-permute-done.25.came_1 = f32[16,4992]{1,0:T(8,128)S(1)} collective-permute-done((f32[16,4992]{1,0:T(8,128)S(1)}, f32[16,4992]{1,0:T(8,128)S(1)}, u32[]{:S(2)}, u32[]{:S(2)}) %collective-permute-start.25) | collective-permute-done | bytes 319520 | tf_op jit(solution)/shard_map/ppermute | solution.py:60
  63.0 4.0 %collective-permute-done.27.came_3 = f32[16,4992]{1,0:T(8,128)S(1)} collective-permute-done((f32[16,4992]{1,0:T(8,128)S(1)}, f32[16,4992]{1,0:T(8,128)S(1)}, u32[]{:S(2)}, u32[]{:S(2)}) %collective-permute-start.27) | collective-permute-done | bytes 319520 | tf_op jit(solution)/shard_map/ppermute | solution.py:60
  67.9 1.7 %collective-permute-start.29 = (bf16[16,4992]{1,0:T(8,128)(2,1)S(1)}, bf16[16,4992]{1,0:T(8,128)(2,1)S(1)}, u32[]{:S(2)}, u32[]{:S(2)}) collective-permute-start(bf16[16,4992]{1,0:T(8,128)(2,1)S(1)} %shard_map.162.refs_0_), channel_id=1, source_target_pairs={{0,64},{1,17},{2,66},{3,19},{4,68},{5,21},{6,70},{7,23},{8,72},{9,... | collective-permute-start | bytes 479240 | tf_op jit(solution)/shard_map/ppermute | solution.py:60
  69.7 1.3 collective-permute-start.28
  71.0 2.9 %collective-permute-done.12.came_3 = f32[16,4992]{1,0:T(8,128)S(1)} collective-permute-done((f32[16,4992]{1,0:T(8,128)S(1)}, f32[16,4992]{1,0:T(8,128)S(1)}, u32[]{:S(2)}, u32[]{:S(2)}) %collective-permute-start.12) | collective-permute-done | bytes 319520 | tf_op jit(solution)/shard_map/ppermute | solution.py:60
  74.8 1.7 %collective-permute-start.14 = (bf16[16,4992]{1,0:T(8,128)(2,1)S(1)}, bf16[16,4992]{1,0:T(8,128)(2,1)S(1)}, u32[]{:S(2)}, u32[]{:S(2)}) collective-permute-start(bf16[16,4992]{1,0:T(8,128)(2,1)S(1)} %shard_map.156.refs_0_), channel_id=1, source_target_pairs={{0,64},{1,17},{2,66},{3,19},{4,68},{5,21},{6,70},{7,23},{8,72},{9,... | collective-permute-start | bytes 479240 | tf_op jit(solution)/shard_map/ppermute | solution.py:60
  76.5 1.0 collective-permute-start.13
  77.5 2.8 %collective-permute-start.31 = (bf16[64,2560]{1,0:T(8,128)(2,1)S(1)}, bf16[64,2560]{1,0:T(8,128)(2,1)S(1)}, u32[]{:S(2)}, u32[]{:S(2)}) collective-permute-start(bf16[64,2560]{1,0:T(8,128)(2,1)S(1)} %get-tuple-element.142.a), channel_id=1, source_target_pairs={{0,48},{1,193},{2,50},{3,195},{4,52},{5,197},{6,54},{7,199},{8,56}... | collective-permute-start | bytes 983048 | tf_op jit(solution)/shard_map/ppermute | solution.py:60
  80.4 0.8 collective-permute-done.14.refs_2_
  82.0 3.0 %collective-permute-start.16 = (bf16[64,2560]{1,0:T(8,128)(2,1)S(1)}, bf16[64,2560]{1,0:T(8,128)(2,1)S(1)}, u32[]{:S(2)}, u32[]{:S(2)}) collective-permute-start(bf16[64,2560]{1,0:T(8,128)(2,1)S(1)} %get-tuple-element.121.a), channel_id=1, source_target_pairs={{0,48},{1,193},{2,50},{3,195},{4,52},{5,197},{6,54},{7,199},{8,56}... | collective-permute-start | bytes 983048 | tf_op jit(solution)/shard_map/ppermute | solution.py:60
  85.0 2.5 %collective-permute-done.32.came_b = bf16[64,2432]{1,0:T(8,128)(2,1)S(1)} collective-permute-done((bf16[64,2432]{1,0:T(8,128)(2,1)S(1)}, bf16[64,2432]{1,0:T(8,128)(2,1)S(1)}, u32[]{:S(2)}, u32[]{:S(2)}) %collective-permute-start.32) | collective-permute-done | bytes 311328 | tf_op jit(solution)/shard_map/ppermute | solution.py:60
  87.6 0.8 collective-permute-start.33
  88.4 1.9 %collective-permute-start.34 = (bf16[128,2432]{1,0:T(8,128)(2,1)S(1)}, bf16[128,2432]{1,0:T(8,128)(2,1)S(1)}, u32[]{:S(2)}, u32[]{:S(2)}) collective-permute-start(bf16[128,2432]{1,0:T(8,128)(2,1)S(1)} %get-tuple-element.145.b.refs_6_), channel_id=1, source_target_pairs={{0,48},{1,193},{2,50},{3,195},{4,52},{5,197},{6,54},{7,199},{8,56}... | collective-permute-start | bytes 1867784 | tf_op jit(solution)/shard_map/ppermute | solution.py:60
  90.9 0.8 collective-permute-start.18
  91.7 2.4 %collective-permute-start.19 = (bf16[128,2432]{1,0:T(8,128)(2,1)S(1)}, bf16[128,2432]{1,0:T(8,128)(2,1)S(1)}, u32[]{:S(2)}, u32[]{:S(2)}) collective-permute-start(bf16[128,2432]{1,0:T(8,128)(2,1)S(1)} %get-tuple-element.124.b.refs_4_), channel_id=1, source_target_pairs={{0,48},{1,193},{2,50},{3,195},{4,52},{5,197},{6,54},{7,199},{8,56}... | collective-permute-start | bytes 1867784 | tf_op jit(solution)/shard_map/ppermute | solution.py:60
  94.1 4.9 %collective-permute-done.34.came_b.refs_7_ = bf16[128,2432]{1,0:T(8,128)(2,1)S(1)} collective-permute-done((bf16[128,2432]{1,0:T(8,128)(2,1)S(1)}, bf16[128,2432]{1,0:T(8,128)(2,1)S(1)}, u32[]{:S(2)}, u32[]{:S(2)}) %collective-permute-start.34) | collective-permute-done | bytes 622624 | tf_op jit(solution)/shard_map/ppermute | solution.py:60
  99.0 2.2 %shard_map.165 = (f32[128,1024]{1,0:T(8,128)S(1)}, f32[128,1024]{1,0:T(8,128)S(1)}) custom-call(s32[16]{0:T(128)S(1)} %get-tuple-element.96.index_a, s32[16]{0:T(128)S(1)} %get-tuple-element.97.index_b, bf16[128,2560]{1,0:T(8,128)(2,1)S(1)} %get-tuple-element.144.a.refs_2_, bf16[128,2560]{1,0:T(8,128)(2,1)S(1)} %collective-permute-done.33.came_a.refs_3_, ...), custom_call_target="tpu_custom_call" | custom-call | flops 1308622848 | bytes 8716416 | tf_op jit(solution)/shard_map/pallas_call | solution.py:85
  101.2 4.9 %collective-permute-start.35 = (f32[128,1024]{1,0:T(8,128)S(1)}, f32[128,1024]{1,0:T(8,128)S(1)}, u32[]{:S(2)}, u32[]{:S(2)}) collective-permute-start(f32[128,1024]{1,0:T(8,128)S(1)} %get-tuple-element.147), channel_id=1, source_target_pairs={{0,1},{1,0},{2,3},{3,2},{4,5},{5,4},{6,7},{7,6},{8,9},{9,8},{10,11... | collective-permute-start | bytes 1572872 | tf_op jit(solution)/shard_map/ppermute | solution.py:436
  106.1 2.2 %shard_map.159 = (f32[128,1024]{1,0:T(8,128)S(1)}, f32[128,1024]{1,0:T(8,128)S(1)}) custom-call(s32[16]{0:T(128)S(1)} %get-tuple-element.96.index_a, s32[16]{0:T(128)S(1)} %get-tuple-element.97.index_b, bf16[128,2560]{1,0:T(8,128)(2,1)S(1)} %get-tuple-element.123.a.refs_0_, bf16[128,2560]{1,0:T(8,128)(2,1)S(1)} %collective-permute-done.18.came_a.refs_1_, ...), custom_call_target="tpu_custom_call" | custom-call | flops 1308622848 | bytes 8716416 | tf_op jit(solution)/shard_map/pallas_call | solution.py:85
  108.4 4.8 %collective-permute-start.20 = (f32[128,1024]{1,0:T(8,128)S(1)}, f32[128,1024]{1,0:T(8,128)S(1)}, u32[]{:S(2)}, u32[]{:S(2)}) collective-permute-start(f32[128,1024]{1,0:T(8,128)S(1)} %get-tuple-element.129), channel_id=1, source_target_pairs={{0,1},{1,0},{2,3},{3,2},{4,5},{5,4},{6,7},{7,6},{8,9},{9,8},{10,11... | collective-permute-start | bytes 1572872 | tf_op jit(solution)/shard_map/ppermute | solution.py:436
  113.1 1.5 %collective-permute-done.20.came_0 = f32[128,1024]{1,0:T(8,128)S(1)} collective-permute-done((f32[128,1024]{1,0:T(8,128)S(1)}, f32[128,1024]{1,0:T(8,128)S(1)}, u32[]{:S(2)}, u32[]{:S(2)}) %collective-permute-start.20) | collective-permute-done | bytes 524320 | tf_op jit(solution)/shard_map/ppermute | solution.py:436
  114.8 3.0 %collective-permute-start.39 = (bf16[32,1024]{1,0:T(8,128)(2,1)S(1)}, bf16[32,1024]{1,0:T(8,128)(2,1)S(1)}, u32[]{:S(2)}, u32[]{:S(2)}) collective-permute-start(bf16[32,1024]{1,0:T(8,128)(2,1)S(1)} %get-tuple-element.161), channel_id=1, source_target_pairs={{0,8},{1,9},{2,10},{3,11},{4,12},{5,13},{6,14},{7,15},{8,0},{9,1},... | collective-permute-start | bytes 196616 | tf_op jit(solution)/shard_map/ppermute | solution.py:442
  117.8 1.9 %collective-permute-start.36 = (bf16[64,1024]{1,0:T(8,128)(2,1)S(1)}, bf16[64,1024]{1,0:T(8,128)(2,1)S(1)}, u32[]{:S(2)}, u32[]{:S(2)}) collective-permute-start(bf16[64,1024]{1,0:T(8,128)(2,1)S(1)} %get-tuple-element.158), channel_id=1, source_target_pairs={{0,2},{1,15},{2,4},{3,1},{4,6},{5,3},{6,8},{7,5},{8,10},{9,7},{10,... | collective-permute-start | bytes 393224 | tf_op jit(solution)/shard_map/ppermute | solution.py:441
  120.2 1.2 collective-permute-start.38
  121.4 6.1 %shard_map.167 = (bf16[512,1664]{1,0:T(8,128)(2,1)}, bf16[512,1664]{1,0:T(8,128)(2,1)}, bf16[1664,512]{1,0:T(8,128)(2,1)}) custom-call(bf16[512,512]{1,0:T(8,128)(2,1)S(1)} %get-tuple-element.150.tokens_a, bf16[512,512]{1,0:T(8,128)(2,1)S(1)} %get-tuple-element.151.tokens_b, bf16[512,512]{1,0:T(8,128)(2,1)S(1)} %get-tuple-element.152.grads_a, ...), custom_call_target="tpu_custom_call" | custom-call | flops 2617245696 | bytes 12320768 | tf_op jit(solution)/shard_map/pallas_call | solution.py:85
  128.3 5.1 %collective-permute-start.40 = (f32[32,1024]{1,0:T(8,128)S(1)}, f32[32,1024]{1,0:T(8,128)S(1)}, u32[]{:S(2)}, u32[]{:S(2)}) collective-permute-start(f32[32,1024]{1,0:T(8,128)S(1)} %get-tuple-element.163), channel_id=1, source_target_pairs={{0,1},{1,0},{2,3},{3,2},{4,5},{5,4},{6,7},{7,6},{8,9},{9,8},{10,11... | collective-permute-start | bytes 393224 | tf_op jit(solution)/shard_map/ppermute | solution.py:452
  133.3 1.0 collective-permute-done.40.came
  (76 shorter events, 14.1 us)
Async XLA Ops:
  0.6 0.8 copy-start.3
  1.4 0.8 copy-start.4
  2.1 19.5 %copy-start.5 = (f32[4,13]{1,0:T(4,128)S(1)}, f32[4,13]{1,0:T(4,128)}, u32[]{:S(2)}) copy-start(f32[4,13]{1,0:T(4,128)} %scale.2) | copy-start | bytes 628
  2.2 8.5 %collective-permute-start.1 = (bf16[64,512]{1,0:T(8,128)(2,1)S(1)}, bf16[64,512]{1,0:T(8,128)(2,1)S(1)}, u32[]{:S(2)}, u32[]{:S(2)}) collective-permute-start(bf16[64,512]{1,0:T(8,128)(2,1)S(1)} %shard_map.146.both), channel_id=1, source_target_pairs={{0,1},{1,0},{2,3},{3,2},{4,5},{5,4},{6,7},{7,6},{8,9},{9,8},{10,11... | collective-permute-start | bytes 196616 | tf_op jit(solution)/shard_map/ppermute | solution.py:373
  5.5 19.3 %collective-permute-start = (bf16[64,512]{1,0:T(8,128)(2,1)S(1)}, bf16[64,512]{1,0:T(8,128)(2,1)S(1)}, u32[]{:S(2)}, u32[]{:S(2)}) collective-permute-start(bf16[64,512]{1,0:T(8,128)(2,1)S(1)} %shard_map.146.both), channel_id=1, source_target_pairs={{0,8},{1,9},{2,10},{3,11},{4,12},{5,13},{6,14},{7,15},{8,0},{9,1},... | collective-permute-start | bytes 196616 | tf_op jit(solution)/shard_map/ppermute | solution.py:375
  10.7 14.1 %collective-permute-start.4 = (bf16[128,512]{1,0:T(8,128)(2,1)S(1)}, bf16[128,512]{1,0:T(8,128)(2,1)S(1)}, u32[]{:S(2)}, u32[]{:S(2)}) collective-permute-start(bf16[128,512]{1,0:T(8,128)(2,1)S(1)} %shard_map.147.pair), channel_id=1, source_target_pairs={{0,6},{1,11},{2,8},{3,13},{4,10},{5,15},{6,12},{7,1},{8,14},{9,3},... | collective-permute-start | bytes 393224 | tf_op jit(solution)/shard_map/ppermute | solution.py:374
  11.2 13.6 %collective-permute-start.3 = (bf16[128,512]{1,0:T(8,128)(2,1)S(1)}, bf16[128,512]{1,0:T(8,128)(2,1)S(1)}, u32[]{:S(2)}, u32[]{:S(2)}) collective-permute-start(bf16[128,512]{1,0:T(8,128)(2,1)S(1)} %shard_map.147.pair), channel_id=1, source_target_pairs={{0,4},{1,13},{2,6},{3,15},{4,8},{5,1},{6,10},{7,3},{8,12},{9,5},{1... | collective-permute-start | bytes 393224 | tf_op jit(solution)/shard_map/ppermute | solution.py:374
  14.8 10.0 %collective-permute-start.2 = (bf16[128,512]{1,0:T(8,128)(2,1)S(1)}, bf16[128,512]{1,0:T(8,128)(2,1)S(1)}, u32[]{:S(2)}, u32[]{:S(2)}) collective-permute-start(bf16[128,512]{1,0:T(8,128)(2,1)S(1)} %shard_map.147.pair), channel_id=1, source_target_pairs={{0,2},{1,15},{2,4},{3,1},{4,6},{5,3},{6,8},{7,5},{8,10},{9,7},{10,... | collective-permute-start | bytes 393224 | tf_op jit(solution)/shard_map/ppermute | solution.py:374
  18.9 1.5 %copy-start = (bf16[1664,512]{1,0:T(8,128)(2,1)S(1)}, bf16[1664,512]{1,0:T(8,128)(2,1)}, u32[]{:S(2)}) copy-start(bf16[1664,512]{1,0:T(8,128)(2,1)} %quant.2) | copy-start | bytes 5111812
  20.4 1.5 %copy-start.1 = (bf16[512,1664]{1,0:T(8,128)(2,1)S(1)}, bf16[512,1664]{1,0:T(8,128)(2,1)}, u32[]{:S(2)}) copy-start(bf16[512,1664]{1,0:T(8,128)(2,1)} %quant) | copy-start | bytes 5111812
  20.4 2.6 %copy-start.2 = (bf16[512,1664]{1,0:T(8,128)(2,1)S(1)}, bf16[512,1664]{1,0:T(8,128)(2,1)}, u32[]{:S(2)}) copy-start(bf16[512,1664]{1,0:T(8,128)(2,1)} %quant.1) | copy-start | bytes 5111812
  20.4 2.6 %copy-start.6 = (f32[4,13]{1,0:T(4,128)S(1)}, f32[4,13]{1,0:T(4,128)}, u32[]{:S(2)}) copy-start(f32[4,13]{1,0:T(4,128)} %scale.3) | copy-start | bytes 628
  24.9 1.9 %collective-permute-start.5 = (bf16[448,512]{1,0:T(8,128)(2,1)S(1)}, bf16[448,512]{1,0:T(8,128)(2,1)S(1)}, u32[]{:S(2)}, u32[]{:S(2)}) collective-permute-start(bf16[448,512]{1,0:T(8,128)(2,1)S(1)} %shard_map.151), channel_id=1, source_target_pairs={{0,1},{1,0},{2,3},{3,2},{4,5},{5,4},{6,7},{7,6},{8,9},{9,8},{10,11... | collective-permute-start | bytes 1376264 | tf_op jit(solution)/shard_map/ppermute | solution.py:411
  30.6 12.0 %collective-permute-start.21 = (bf16[128,2560]{1,0:T(8,128)(2,1)S(1)}, bf16[128,2560]{1,0:T(8,128)(2,1)S(1)}, u32[]{:S(2)}, u32[]{:S(2)}) collective-permute-start(bf16[128,2560]{1,0:T(8,128)(2,1)S(1)} %get-tuple-element.131), channel_id=1, source_target_pairs={{0,16},{1,65},{2,18},{3,67},{4,20},{5,69},{6,22},{7,71},{8,24},{9,... | collective-permute-start | bytes 1966088 | tf_op jit(solution)/shard_map/ppermute | solution.py:60
  32.0 10.6 %collective-permute-start.22 = (bf16[128,2432]{1,0:T(8,128)(2,1)S(1)}, bf16[128,2432]{1,0:T(8,128)(2,1)S(1)}, u32[]{:S(2)}, u32[]{:S(2)}) collective-permute-start(bf16[128,2432]{1,0:T(8,128)(2,1)S(1)} %get-tuple-element.133), channel_id=1, source_target_pairs={{0,48},{1,193},{2,50},{3,195},{4,52},{5,197},{6,54},{7,199},{8,56}... | collective-permute-start | bytes 1867784 | tf_op jit(solution)/shard_map/ppermute | solution.py:60
  33.9 15.4 %collective-permute-start.6 = (bf16[128,2560]{1,0:T(8,128)(2,1)S(1)}, bf16[128,2560]{1,0:T(8,128)(2,1)S(1)}, u32[]{:S(2)}, u32[]{:S(2)}) collective-permute-start(bf16[128,2560]{1,0:T(8,128)(2,1)S(1)} %get-tuple-element.110), channel_id=1, source_target_pairs={{0,16},{1,65},{2,18},{3,67},{4,20},{5,69},{6,22},{7,71},{8,24},{9,... | collective-permute-start | bytes 1966088 | tf_op jit(solution)/shard_map/ppermute | solution.py:60
  34.3 15.0 %collective-permute-start.7 = (bf16[128,2432]{1,0:T(8,128)(2,1)S(1)}, bf16[128,2432]{1,0:T(8,128)(2,1)S(1)}, u32[]{:S(2)}, u32[]{:S(2)}) collective-permute-start(bf16[128,2432]{1,0:T(8,128)(2,1)S(1)} %get-tuple-element.112), channel_id=1, source_target_pairs={{0,48},{1,193},{2,50},{3,195},{4,52},{5,197},{6,54},{7,199},{8,56}... | collective-permute-start | bytes 1867784 | tf_op jit(solution)/shard_map/ppermute | solution.py:60
  42.8 10.0 %collective-permute-start.23 = (bf16[64,2560]{1,0:T(8,128)(2,1)S(1)}, bf16[64,2560]{1,0:T(8,128)(2,1)S(1)}, u32[]{:S(2)}, u32[]{:S(2)}) collective-permute-start(bf16[64,2560]{1,0:T(8,128)(2,1)S(1)} %get-tuple-element.135), channel_id=1, source_target_pairs={{0,48},{1,193},{2,50},{3,195},{4,52},{5,197},{6,54},{7,199},{8,56}... | collective-permute-start | bytes 983048 | tf_op jit(solution)/shard_map/ppermute | solution.py:60
  44.8 6.7 %collective-permute-start.24 = (bf16[64,2432]{1,0:T(8,128)(2,1)S(1)}, bf16[64,2432]{1,0:T(8,128)(2,1)S(1)}, u32[]{:S(2)}, u32[]{:S(2)}) collective-permute-start(bf16[64,2432]{1,0:T(8,128)(2,1)S(1)} %get-tuple-element.137), channel_id=1, source_target_pairs={{0,16},{1,65},{2,18},{3,67},{4,20},{5,69},{6,22},{7,71},{8,24},{9,... | collective-permute-start | bytes 933896 | tf_op jit(solution)/shard_map/ppermute | solution.py:60
  49.5 8.0 %collective-permute-start.8 = (bf16[64,2560]{1,0:T(8,128)(2,1)S(1)}, bf16[64,2560]{1,0:T(8,128)(2,1)S(1)}, u32[]{:S(2)}, u32[]{:S(2)}) collective-permute-start(bf16[64,2560]{1,0:T(8,128)(2,1)S(1)} %get-tuple-element.114), channel_id=1, source_target_pairs={{0,48},{1,193},{2,50},{3,195},{4,52},{5,197},{6,54},{7,199},{8,56}... | collective-permute-start | bytes 983048 | tf_op jit(solution)/shard_map/ppermute | solution.py:60
  51.5 6.0 %collective-permute-start.9 = (bf16[64,2432]{1,0:T(8,128)(2,1)S(1)}, bf16[64,2432]{1,0:T(8,128)(2,1)S(1)}, u32[]{:S(2)}, u32[]{:S(2)}) collective-permute-start(bf16[64,2432]{1,0:T(8,128)(2,1)S(1)} %get-tuple-element.116), channel_id=1, source_target_pairs={{0,16},{1,65},{2,18},{3,67},{4,20},{5,69},{6,22},{7,71},{8,24},{9,... | collective-permute-start | bytes 933896 | tf_op jit(solution)/shard_map/ppermute | solution.py:60
  52.9 9.3 %collective-permute-start.25 = (f32[16,4992]{1,0:T(8,128)S(1)}, f32[16,4992]{1,0:T(8,128)S(1)}, u32[]{:S(2)}, u32[]{:S(2)}) collective-permute-start(f32[16,4992]{1,0:T(8,128)S(1)} %get-tuple-element.139), channel_id=1, source_target_pairs={{0,192},{1,49},{2,194},{3,51},{4,196},{5,53},{6,198},{7,55},{8,200... | collective-permute-start | bytes 958472 | tf_op jit(solution)/shard_map/ppermute | solution.py:60
  55.5 7.5 %collective-permute-start.26 = (f32[16,4992]{1,0:T(8,128)S(1)}, f32[16,4992]{1,0:T(8,128)S(1)}, u32[]{:S(2)}, u32[]{:S(2)}) collective-permute-start(f32[16,4992]{1,0:T(8,128)S(1)} %get-tuple-element.140), channel_id=1, source_target_pairs={{0,64},{1,17},{2,66},{3,19},{4,68},{5,21},{6,70},{7,23},{8,72},{9,... | collective-permute-start | bytes 958472 | tf_op jit(solution)/shard_map/ppermute | solution.py:60
  55.5 11.6 %collective-permute-start.27 = (f32[16,4992]{1,0:T(8,128)S(1)}, f32[16,4992]{1,0:T(8,128)S(1)}, u32[]{:S(2)}, u32[]{:S(2)}) collective-permute-start(f32[16,4992]{1,0:T(8,128)S(1)} %get-tuple-element.141), channel_id=1, source_target_pairs={{0,128},{1,33},{2,130},{3,35},{4,132},{5,37},{6,134},{7,39},{8,136... | collective-permute-start | bytes 958472 | tf_op jit(solution)/shard_map/ppermute | solution.py:60
  57.6 12.0 %collective-permute-start.10 = (f32[16,4992]{1,0:T(8,128)S(1)}, f32[16,4992]{1,0:T(8,128)S(1)}, u32[]{:S(2)}, u32[]{:S(2)}) collective-permute-start(f32[16,4992]{1,0:T(8,128)S(1)} %get-tuple-element.118), channel_id=1, source_target_pairs={{0,192},{1,49},{2,194},{3,51},{4,196},{5,53},{6,198},{7,55},{8,200... | collective-permute-start | bytes 958472 | tf_op jit(solution)/shard_map/ppermute | solution.py:60
  60.2 10.8 %collective-permute-start.11 = (f32[16,4992]{1,0:T(8,128)S(1)}, f32[16,4992]{1,0:T(8,128)S(1)}, u32[]{:S(2)}, u32[]{:S(2)}) collective-permute-start(f32[16,4992]{1,0:T(8,128)S(1)} %get-tuple-element.119), channel_id=1, source_target_pairs={{0,64},{1,17},{2,66},{3,19},{4,68},{5,21},{6,70},{7,23},{8,72},{9,... | collective-permute-start | bytes 958472 | tf_op jit(solution)/shard_map/ppermute | solution.py:60
  62.2 11.7 %collective-permute-start.12 = (f32[16,4992]{1,0:T(8,128)S(1)}, f32[16,4992]{1,0:T(8,128)S(1)}, u32[]{:S(2)}, u32[]{:S(2)}) collective-permute-start(f32[16,4992]{1,0:T(8,128)S(1)} %get-tuple-element.120), channel_id=1, source_target_pairs={{0,128},{1,33},{2,130},{3,35},{4,132},{5,37},{6,134},{7,39},{8,136... | collective-permute-start | bytes 958472 | tf_op jit(solution)/shard_map/ppermute | solution.py:60
  67.2 9.3 %collective-permute-start.30 = (bf16[16,4992]{1,0:T(8,128)(2,1)S(1)}, bf16[16,4992]{1,0:T(8,128)(2,1)S(1)}, u32[]{:S(2)}, u32[]{:S(2)}) collective-permute-start(bf16[16,4992]{1,0:T(8,128)(2,1)S(1)} %shard_map.162.refs_0_), channel_id=1, source_target_pairs={{0,128},{1,33},{2,130},{3,35},{4,132},{5,37},{6,134},{7,39},{8,136... | collective-permute-start | bytes 479240 | tf_op jit(solution)/shard_map/ppermute | solution.py:60
  67.9 9.6 %collective-permute-start.29 = (bf16[16,4992]{1,0:T(8,128)(2,1)S(1)}, bf16[16,4992]{1,0:T(8,128)(2,1)S(1)}, u32[]{:S(2)}, u32[]{:S(2)}) collective-permute-start(bf16[16,4992]{1,0:T(8,128)(2,1)S(1)} %shard_map.162.refs_0_), channel_id=1, source_target_pairs={{0,64},{1,17},{2,66},{3,19},{4,68},{5,21},{6,70},{7,23},{8,72},{9,... | collective-permute-start | bytes 479240 | tf_op jit(solution)/shard_map/ppermute | solution.py:60
  69.7 7.8 %collective-permute-start.28 = (bf16[16,4992]{1,0:T(8,128)(2,1)S(1)}, bf16[16,4992]{1,0:T(8,128)(2,1)S(1)}, u32[]{:S(2)}, u32[]{:S(2)}) collective-permute-start(bf16[16,4992]{1,0:T(8,128)(2,1)S(1)} %shard_map.162.refs_0_), channel_id=1, source_target_pairs={{0,192},{1,49},{2,194},{3,51},{4,196},{5,53},{6,198},{7,55},{8,200... | collective-permute-start | bytes 479240 | tf_op jit(solution)/shard_map/ppermute | solution.py:60
  74.0 6.3 %collective-permute-start.15 = (bf16[16,4992]{1,0:T(8,128)(2,1)S(1)}, bf16[16,4992]{1,0:T(8,128)(2,1)S(1)}, u32[]{:S(2)}, u32[]{:S(2)}) collective-permute-start(bf16[16,4992]{1,0:T(8,128)(2,1)S(1)} %shard_map.156.refs_0_), channel_id=1, source_target_pairs={{0,128},{1,33},{2,130},{3,35},{4,132},{5,37},{6,134},{7,39},{8,136... | collective-permute-start | bytes 479240 | tf_op jit(solution)/shard_map/ppermute | solution.py:60
  74.8 6.4 %collective-permute-start.14 = (bf16[16,4992]{1,0:T(8,128)(2,1)S(1)}, bf16[16,4992]{1,0:T(8,128)(2,1)S(1)}, u32[]{:S(2)}, u32[]{:S(2)}) collective-permute-start(bf16[16,4992]{1,0:T(8,128)(2,1)S(1)} %shard_map.156.refs_0_), channel_id=1, source_target_pairs={{0,64},{1,17},{2,66},{3,19},{4,68},{5,21},{6,70},{7,23},{8,72},{9,... | collective-permute-start | bytes 479240 | tf_op jit(solution)/shard_map/ppermute | solution.py:60
  76.5 5.5 %collective-permute-start.13 = (bf16[16,4992]{1,0:T(8,128)(2,1)S(1)}, bf16[16,4992]{1,0:T(8,128)(2,1)S(1)}, u32[]{:S(2)}, u32[]{:S(2)}) collective-permute-start(bf16[16,4992]{1,0:T(8,128)(2,1)S(1)} %shard_map.156.refs_0_), channel_id=1, source_target_pairs={{0,192},{1,49},{2,194},{3,51},{4,196},{5,53},{6,198},{7,55},{8,200... | collective-permute-start | bytes 479240 | tf_op jit(solution)/shard_map/ppermute | solution.py:60
  77.5 9.9 %collective-permute-start.31 = (bf16[64,2560]{1,0:T(8,128)(2,1)S(1)}, bf16[64,2560]{1,0:T(8,128)(2,1)S(1)}, u32[]{:S(2)}, u32[]{:S(2)}) collective-permute-start(bf16[64,2560]{1,0:T(8,128)(2,1)S(1)} %get-tuple-element.142.a), channel_id=1, source_target_pairs={{0,48},{1,193},{2,50},{3,195},{4,52},{5,197},{6,54},{7,199},{8,56}... | collective-permute-start | bytes 983048 | tf_op jit(solution)/shard_map/ppermute | solution.py:60
  80.4 7.1 %collective-permute-start.32 = (bf16[64,2432]{1,0:T(8,128)(2,1)S(1)}, bf16[64,2432]{1,0:T(8,128)(2,1)S(1)}, u32[]{:S(2)}, u32[]{:S(2)}) collective-permute-start(bf16[64,2432]{1,0:T(8,128)(2,1)S(1)} %get-tuple-element.143.b), channel_id=1, source_target_pairs={{0,16},{1,65},{2,18},{3,67},{4,20},{5,69},{6,22},{7,71},{8,24},{9,... | collective-permute-start | bytes 933896 | tf_op jit(solution)/shard_map/ppermute | solution.py:60
  82.0 8.8 %collective-permute-start.16 = (bf16[64,2560]{1,0:T(8,128)(2,1)S(1)}, bf16[64,2560]{1,0:T(8,128)(2,1)S(1)}, u32[]{:S(2)}, u32[]{:S(2)}) collective-permute-start(bf16[64,2560]{1,0:T(8,128)(2,1)S(1)} %get-tuple-element.121.a), channel_id=1, source_target_pairs={{0,48},{1,193},{2,50},{3,195},{4,52},{5,197},{6,54},{7,199},{8,56}... | collective-permute-start | bytes 983048 | tf_op jit(solution)/shard_map/ppermute | solution.py:60
  85.0 5.7 %collective-permute-start.17 = (bf16[64,2432]{1,0:T(8,128)(2,1)S(1)}, bf16[64,2432]{1,0:T(8,128)(2,1)S(1)}, u32[]{:S(2)}, u32[]{:S(2)}) collective-permute-start(bf16[64,2432]{1,0:T(8,128)(2,1)S(1)} %get-tuple-element.122.b), channel_id=1, source_target_pairs={{0,16},{1,65},{2,18},{3,67},{4,20},{5,69},{6,22},{7,71},{8,24},{9,... | collective-permute-start | bytes 933896 | tf_op jit(solution)/shard_map/ppermute | solution.py:60
  87.6 11.4 %collective-permute-start.33 = (bf16[128,2560]{1,0:T(8,128)(2,1)S(1)}, bf16[128,2560]{1,0:T(8,128)(2,1)S(1)}, u32[]{:S(2)}, u32[]{:S(2)}) collective-permute-start(bf16[128,2560]{1,0:T(8,128)(2,1)S(1)} %get-tuple-element.144.a.refs_2_), channel_id=1, source_target_pairs={{0,16},{1,65},{2,18},{3,67},{4,20},{5,69},{6,22},{7,71},{8,24},{9,... | collective-permute-start | bytes 1966088 | tf_op jit(solution)/shard_map/ppermute | solution.py:60
  88.4 10.6 %collective-permute-start.34 = (bf16[128,2432]{1,0:T(8,128)(2,1)S(1)}, bf16[128,2432]{1,0:T(8,128)(2,1)S(1)}, u32[]{:S(2)}, u32[]{:S(2)}) collective-permute-start(bf16[128,2432]{1,0:T(8,128)(2,1)S(1)} %get-tuple-element.145.b.refs_6_), channel_id=1, source_target_pairs={{0,48},{1,193},{2,50},{3,195},{4,52},{5,197},{6,54},{7,199},{8,56}... | collective-permute-start | bytes 1867784 | tf_op jit(solution)/shard_map/ppermute | solution.py:60
  90.9 15.3 %collective-permute-start.18 = (bf16[128,2560]{1,0:T(8,128)(2,1)S(1)}, bf16[128,2560]{1,0:T(8,128)(2,1)S(1)}, u32[]{:S(2)}, u32[]{:S(2)}) collective-permute-start(bf16[128,2560]{1,0:T(8,128)(2,1)S(1)} %get-tuple-element.123.a.refs_0_), channel_id=1, source_target_pairs={{0,16},{1,65},{2,18},{3,67},{4,20},{5,69},{6,22},{7,71},{8,24},{9,... | collective-permute-start | bytes 1966088 | tf_op jit(solution)/shard_map/ppermute | solution.py:60
  91.7 14.5 %collective-permute-start.19 = (bf16[128,2432]{1,0:T(8,128)(2,1)S(1)}, bf16[128,2432]{1,0:T(8,128)(2,1)S(1)}, u32[]{:S(2)}, u32[]{:S(2)}) collective-permute-start(bf16[128,2432]{1,0:T(8,128)(2,1)S(1)} %get-tuple-element.124.b.refs_4_), channel_id=1, source_target_pairs={{0,48},{1,193},{2,50},{3,195},{4,52},{5,197},{6,54},{7,199},{8,56}... | collective-permute-start | bytes 1867784 | tf_op jit(solution)/shard_map/ppermute | solution.py:60
  101.2 11.9 %collective-permute-start.35 = (f32[128,1024]{1,0:T(8,128)S(1)}, f32[128,1024]{1,0:T(8,128)S(1)}, u32[]{:S(2)}, u32[]{:S(2)}) collective-permute-start(f32[128,1024]{1,0:T(8,128)S(1)} %get-tuple-element.147), channel_id=1, source_target_pairs={{0,1},{1,0},{2,3},{3,2},{4,5},{5,4},{6,7},{7,6},{8,9},{9,8},{10,11... | collective-permute-start | bytes 1572872 | tf_op jit(solution)/shard_map/ppermute | solution.py:436
  108.4 6.3 %collective-permute-start.20 = (f32[128,1024]{1,0:T(8,128)S(1)}, f32[128,1024]{1,0:T(8,128)S(1)}, u32[]{:S(2)}, u32[]{:S(2)}) collective-permute-start(f32[128,1024]{1,0:T(8,128)S(1)} %get-tuple-element.129), channel_id=1, source_target_pairs={{0,1},{1,0},{2,3},{3,2},{4,5},{5,4},{6,7},{7,6},{8,9},{9,8},{10,11... | collective-permute-start | bytes 1572872 | tf_op jit(solution)/shard_map/ppermute | solution.py:436
  114.8 12.6 %collective-permute-start.39 = (bf16[32,1024]{1,0:T(8,128)(2,1)S(1)}, bf16[32,1024]{1,0:T(8,128)(2,1)S(1)}, u32[]{:S(2)}, u32[]{:S(2)}) collective-permute-start(bf16[32,1024]{1,0:T(8,128)(2,1)S(1)} %get-tuple-element.161), channel_id=1, source_target_pairs={{0,8},{1,9},{2,10},{3,11},{4,12},{5,13},{6,14},{7,15},{8,0},{9,1},... | collective-permute-start | bytes 196616 | tf_op jit(solution)/shard_map/ppermute | solution.py:442
  117.8 9.7 %collective-permute-start.36 = (bf16[64,1024]{1,0:T(8,128)(2,1)S(1)}, bf16[64,1024]{1,0:T(8,128)(2,1)S(1)}, u32[]{:S(2)}, u32[]{:S(2)}) collective-permute-start(bf16[64,1024]{1,0:T(8,128)(2,1)S(1)} %get-tuple-element.158), channel_id=1, source_target_pairs={{0,2},{1,15},{2,4},{3,1},{4,6},{5,3},{6,8},{7,5},{8,10},{9,7},{10,... | collective-permute-start | bytes 393224 | tf_op jit(solution)/shard_map/ppermute | solution.py:441
  119.7 8.5 %collective-permute-start.37 = (bf16[64,1024]{1,0:T(8,128)(2,1)S(1)}, bf16[64,1024]{1,0:T(8,128)(2,1)S(1)}, u32[]{:S(2)}, u32[]{:S(2)}) collective-permute-start(bf16[64,1024]{1,0:T(8,128)(2,1)S(1)} %get-tuple-element.159), channel_id=1, source_target_pairs={{0,4},{1,13},{2,6},{3,15},{4,8},{5,1},{6,10},{7,3},{8,12},{9,5},{1... | collective-permute-start | bytes 393224 | tf_op jit(solution)/shard_map/ppermute | solution.py:441
  120.2 8.0 %collective-permute-start.38 = (bf16[64,1024]{1,0:T(8,128)(2,1)S(1)}, bf16[64,1024]{1,0:T(8,128)(2,1)S(1)}, u32[]{:S(2)}, u32[]{:S(2)}) collective-permute-start(bf16[64,1024]{1,0:T(8,128)(2,1)S(1)} %get-tuple-element.160), channel_id=1, source_target_pairs={{0,6},{1,11},{2,8},{3,13},{4,10},{5,15},{6,12},{7,1},{8,14},{9,3},... | collective-permute-start | bytes 393224 | tf_op jit(solution)/shard_map/ppermute | solution.py:441
  128.3 6.0 %collective-permute-start.40 = (f32[32,1024]{1,0:T(8,128)S(1)}, f32[32,1024]{1,0:T(8,128)S(1)}, u32[]{:S(2)}, u32[]{:S(2)}) collective-permute-start(f32[32,1024]{1,0:T(8,128)S(1)} %get-tuple-element.163), channel_id=1, source_target_pairs={{0,1},{1,0},{2,3},{3,2},{4,5},{5,4},{6,7},{7,6},{8,9},{9,8},{10,11... | collective-permute-start | bytes 393224 | tf_op jit(solution)/shard_map/ppermute | solution.py:452
